TPU v7x, 256 devices: a whole 4x4x8 slice. The times are simulated.
256 devices in a mesh: tm: 16 (over y_hi, x, core), rows: 16 (over z, y_lo).
Axes of the slice: x: 4, y: 4 (y_hi: 2, y_lo: 2; y = y_hi * 2 + y_lo), z: 8, core: 2. Of those that a mesh axis runs over, the one named last changes fastest.
Arguments:
- frames: bfloat16 [64, 256, 3072], P('tm', 'rows'), may hold values from -6 to 6
- gain_one: float32 [96], replicated, may hold values from 0.5 to 1.5
- weight_one: bfloat16 [3, 3, 3, 96, 96], replicated, may hold values from -0.125 to 0.125
- bias_one: float32 [96], replicated, may hold values from -1.5 to 1.5
- gain_two: float32 [96], replicated, may hold values from 0.5 to 1.5
- weight_two: bfloat16 [3, 3, 3, 96, 96], replicated, may hold values from -0.125 to 0.125
- bias_two: float32 [96], replicated, may hold values from -1.5 to 1.5
Outputs:
- block_out: bfloat16 [64, 256, 3072], P('tm', 'rows')
All inputs are finite; a program needn't handle non-finite values.
Results may differ from a plain program's by a relative error of at most 0.0047.
Values may be sent and summed in bfloat16 or wider, within the bound.
No kernel may reach another device: no remote copies, remote signals or barrier semaphores. Data moves between devices by JAX's collectives and lax.ppermute only.
A program may use at most 64 MiB of HBM per device.

v0:
```python
import jax
import jax.numpy as jnp
from jax import lax
from jax.sharding import PartitionSpec as P


def shifted(value, axis, by):
    count = lax.axis_size(axis)
    pairs = [(i, i + by) for i in range(count) if 0 <= i + by < count]
    return lax.ppermute(value, axis, pairs)


def with_halo(cells, sides, width):
    for axis, dim in sides:
        count = lax.axis_size(axis)
        ends = count - 1
        head = lax.slice_in_dim(cells, 0, width, axis=dim)
        tail = lax.slice_in_dim(cells, cells.shape[dim] - width, cells.shape[dim], axis=dim)
        cells = jnp.concatenate(
            [
                lax.ppermute(tail, axis, [(i, (i + 1) % count) for i in range(ends)]),
                cells,
                lax.ppermute(head, axis, [((i + 1) % count, i) for i in range(ends)]),
            ],
            axis=dim,
        )
    return cells


def norm_act(value, gain):
    mean_sq = jnp.mean(value * value, axis=-1, keepdims=True)
    return jax.nn.silu(value * lax.rsqrt(mean_sq + 1e-06) * gain)


def conv_local(extended, weight, bias):
    out_frames = extended.shape[0] - 2
    out_rows = extended.shape[1] - 2
    width = extended.shape[2]
    chans = extended.shape[3]
    padded = jnp.pad(extended, ((0, 0), (0, 0), (1, 1), (0, 0)))
    total = jnp.zeros((out_frames, out_rows, width, weight.shape[4]), jnp.float32)
    for step_t in range(3):
        for step_h in range(3):
            slab = padded[step_t : step_t + out_frames, step_h : step_h + out_rows]
            stacked = jnp.concatenate(
                [slab[:, :, 0:width], slab[:, :, 1 : width + 1], slab[:, :, 2 : width + 2]], axis=-1
            )
            kernel = weight[step_t, step_h].reshape(3 * chans, weight.shape[4])
            total = total + jnp.einsum(
                "fhwk,ko->fhwo", stacked, kernel, preferred_element_type=jnp.float32
            )
    return total + bias


def body(frames, gain_one, weight_one, bias_one, gain_two, weight_two, bias_two):
    chans = gain_one.shape[0]
    num_frames = frames.shape[0]
    num_rows = frames.shape[1]
    width = frames.shape[2] // chans
    inputs = frames.reshape(num_frames, num_rows, width, chans)
    act_one = norm_act(inputs.astype(jnp.float32), gain_one).astype(jnp.bfloat16)
    earlier = shifted(act_one[num_frames - 2 :], "tm", 1)
    joined = jnp.concatenate([earlier, act_one], axis=0)
    extended = with_halo(joined, (("rows", 1),), 1)
    hidden = conv_local(extended, weight_one, bias_one).astype(jnp.bfloat16)
    hidden = lax.optimization_barrier(hidden)
    act_two = norm_act(hidden.astype(jnp.float32), gain_two).astype(jnp.bfloat16)
    earlier_two = shifted(act_two[num_frames - 2 :], "tm", 1)
    joined_two = jnp.concatenate([earlier_two, act_two], axis=0)
    extended_two = with_halo(joined_two, (("rows", 1),), 1)
    branch = conv_local(extended_two, weight_two, bias_two)
    result = inputs.astype(jnp.float32) + branch
    return result.astype(jnp.bfloat16).reshape(num_frames, num_rows, width * chans)


def solution(mesh):
    in_specs = (P("tm", "rows", None), P(), P(), P(), P(), P(), P())
    out_specs = P("tm", "rows", None)
    return jax.shard_map(body, mesh=mesh, in_specs=in_specs, out_specs=out_specs, check_vma=False)
```

profile of v0, /device:TPU:120, one launch (start us, length us, event | category | flops | bytes accessed | tf_op | source)
XLA Modules:
  0.0 76.4 jit_solution(4141788348037297034)
XLA Ops:
  0.0 1.4 %reshape.27 = f32[4,16,32,96]{3,2,1,0:T(8,128)S(1)} reshape(bf16[4,16,3072]{2,1,0:T(8,128)(2,1)} %param.7) | data formatting | bytes 1179648 | tf_op jit(solution)/shard_map/convert_element_type | solution.py:72
  1.5 0.3 multiply_reduce_fusion
  1.8 0.0 copy-start
  1.9 0.4 multiply_convert_fusion
  2.3 1.9 %collective-permute-start = (bf16[2,16,32,96]{3,2,1,0:T(8,128)(2,1)S(1)}, bf16[2,16,32,96]{3,2,1,0:T(8,128)(2,1)S(1)}, u32[]{:S(2)}, u32[]{:S(2)}) collective-permute-start(bf16[2,16,32,96]{3,2,1,0:T(8,128)(2,1)S(1)} %slice.414), channel_id=1, source_target_pairs={{0,16},{16,32},{32,48},{48,64},{64,80},{80,96},{96,112},{112,128},... | collective-permute-start | bytes 589832 | tf_op jit(solution)/shard_map/ppermute | solution.py:10
  4.2 9.8 %collective-permute-done = bf16[2,16,32,96]{3,2,1,0:T(8,128)(2,1)S(1)} collective-permute-done((bf16[2,16,32,96]{3,2,1,0:T(8,128)(2,1)S(1)}, bf16[2,16,32,96]{3,2,1,0:T(8,128)(2,1)S(1)}, u32[]{:S(2)}, u32[]{:S(2)}) %collective-permute-start) | collective-permute-done | bytes 196640 | tf_op jit(solution)/shard_map/ppermute | solution.py:10
  14.1 4.8 %collective-permute-start.1 = (bf16[6,1,32,96]{3,2,1,0:T(8,128)(2,1)S(1)}, bf16[6,1,32,96]{3,2,1,0:T(8,128)(2,1)S(1)}, u32[]{:S(2)}, u32[]{:S(2)}) collective-permute-start(bf16[6,1,32,96]{3,2,1,0:T(8,128)(2,1)S(1)} %get-tuple-element.59), channel_id=1, source_target_pairs={{0,1},{1,2},{2,3},{3,4},{4,5},{5,6},{6,7},{7,8},{8,9},{9,10},{10,1... | collective-permute-start | bytes 110600 | tf_op jit(solution)/shard_map/ppermute | solution.py:21
  18.9 1.9 %collective-permute-start.2 = (bf16[6,1,32,96]{3,2,1,0:T(8,128)(2,1)S(1)}, bf16[6,1,32,96]{3,2,1,0:T(8,128)(2,1)S(1)}, u32[]{:S(2)}, u32[]{:S(2)}) collective-permute-start(bf16[6,1,32,96]{3,2,1,0:T(8,128)(2,1)S(1)} %get-tuple-element.60), channel_id=1, source_target_pairs={{1,0},{2,1},{3,2},{4,3},{5,4},{6,5},{7,6},{8,7},{9,8},{10,9},{11,1... | collective-permute-start | bytes 110600 | tf_op jit(solution)/shard_map/ppermute | solution.py:23
  20.8 0.1 fusion.193
  21.0 6.0 %collective-permute-done.2 = bf16[6,1,32,96]{3,2,1,0:T(8,128)(2,1)S(1)} collective-permute-done((bf16[6,1,32,96]{3,2,1,0:T(8,128)(2,1)S(1)}, bf16[6,1,32,96]{3,2,1,0:T(8,128)(2,1)S(1)}, u32[]{:S(2)}, u32[]{:S(2)}) %collective-permute-start.2) | collective-permute-done | bytes 36896 | tf_op jit(solution)/shard_map/ppermute | solution.py:23
  27.0 0.5 fusion.181
  27.5 2.8 %fusion.213 = (bf16[4,16,32,96]{3,2,1,0:T(8,128)(2,1)S(1)}, bf16[4,16,32,96]{3,2,1,0:T(8,128)(2,1)S(1)}, bf16[4,16,32,96]{3,2,1,0:T(8,128)(2,1)S(1)}, bf16[4,16,...) fusion(bf16[6,18,34,96]{3,2,1,0:T(8,128)(2,1)S(1)} %fusion.181), kind=kLoop, calls=%fused_computation.193 | loop fusion | bytes 14155776 | tf_op jit(solution)/shard_map/slice | solution.py:46
  30.3 0.2 pad_maximum_fusion.2
  30.5 0.7 fusion.216
  31.2 0.9 %fusion.49 = f32[4,16,32,96]{3,2,1,0:T(8,128)S(1)} fusion(bf16[288,96,1,1]{1,0,3,2:T(8,128)(2,1)S(1)} %bitcast.127, bf16[4,16,32,96]{3,2,1,0:T(8,128)(2,1)S(1)} %get-tuple-element.24, bf16[4,16,32,96]{3,2,1,0:T(8,128)(2,1)S(1)} %multiply_convert_fusion, bf16[4,16,32,96]{3,2,1,0:T(8,128)(2,1)S(1)} %get-tuple-element.25), kind=kOutput, calls=%fused_computation.51 | convolution fusion | flops 116785152 | bytes 2021376 | tf_op jit(solution)/shard_map/fhwk,ko->fhwo/dot_general | solution.py:49
  32.2 0.9 %fusion.17 = f32[4,16,32,96]{3,2,1,0:T(8,128)S(1)} fusion(bf16[288,96,1,1]{1,0,3,2:T(8,128)(2,1)S(1)} %bitcast.125, bf16[4,16,32,96]{3,2,1,0:T(8,128)(2,1)S(1)} %get-tuple-element.36, bf16[4,16,32,96]{3,2,1,0:T(8,128)(2,1)S(1)} %fusion.193, bf16[4,16,32,96]{3,2,1,0:T(8,128)(2,1)S(1)} %get-tuple-element.37), kind=kOutput, calls=%fused_computation.19 | convolution fusion | flops 116785152 | bytes 2021376 | tf_op jit(solution)/shard_map/fhwk,ko->fhwo/dot_general | solution.py:49
  33.1 0.9 %fusion.23 = f32[4,16,32,96]{3,2,1,0:T(8,128)S(1)} fusion(bf16[288,96,1,1]{1,0,3,2:T(8,128)(2,1)S(1)} %bitcast.123, bf16[4,16,32,96]{3,2,1,0:T(8,128)(2,1)S(1)} %get-tuple-element.34, bf16[4,16,32,96]{3,2,1,0:T(8,128)(2,1)S(1)} %get-tuple-element.49, bf16[4,16,32,96]{3,2,1,0:T(8,128)(2,1)S(1)} %get-tuple-element.35), kind=kOutput, calls=%fused_computation.25 | convolution fusion | flops 116785152 | bytes 2021376 | tf_op jit(solution)/shard_map/fhwk,ko->fhwo/dot_general | solution.py:49
  34.0 0.9 %fusion.29 = f32[4,16,32,96]{3,2,1,0:T(8,128)S(1)} fusion(bf16[288,96,1,1]{1,0,3,2:T(8,128)(2,1)S(1)} %bitcast.121, bf16[4,16,32,96]{3,2,1,0:T(8,128)(2,1)S(1)} %get-tuple-element.32, bf16[4,16,32,96]{3,2,1,0:T(8,128)(2,1)S(1)} %get-tuple-element.79, bf16[4,16,32,96]{3,2,1,0:T(8,128)(2,1)S(1)} %get-tuple-element.33), kind=kOutput, calls=%fused_computation.31 | convolution fusion | flops 116785152 | bytes 2021376 | tf_op jit(solution)/shard_map/fhwk,ko->fhwo/dot_general | solution.py:49
  35.0 0.9 %fusion.37 = f32[4,16,32,96]{3,2,1,0:T(8,128)S(1)} fusion(bf16[288,96,1,1]{1,0,3,2:T(8,128)(2,1)S(1)} %bitcast.119, bf16[4,16,32,96]{3,2,1,0:T(8,128)(2,1)S(1)} %get-tuple-element.28, bf16[4,16,32,96]{3,2,1,0:T(8,128)(2,1)S(1)} %get-tuple-element.48, bf16[4,16,32,96]{3,2,1,0:T(8,128)(2,1)S(1)} %get-tuple-element.29), kind=kOutput, calls=%fused_computation.39 | convolution fusion | flops 116785152 | bytes 2021376 | tf_op jit(solution)/shard_map/fhwk,ko->fhwo/dot_general | solution.py:49
  35.9 0.9 %fusion.43 = f32[4,16,32,96]{3,2,1,0:T(8,128)S(1)} fusion(bf16[288,96,1,1]{1,0,3,2:T(8,128)(2,1)S(1)} %bitcast.117, bf16[4,16,32,96]{3,2,1,0:T(8,128)(2,1)S(1)} %get-tuple-element.26, bf16[4,16,32,96]{3,2,1,0:T(8,128)(2,1)S(1)} %get-tuple-element.80, bf16[4,16,32,96]{3,2,1,0:T(8,128)(2,1)S(1)} %get-tuple-element.27), kind=kOutput, calls=%fused_computation.45 | convolution fusion | flops 116785152 | bytes 2021376 | tf_op jit(solution)/shard_map/fhwk,ko->fhwo/dot_general | solution.py:49
  36.8 0.9 %fusion.8 = f32[4,16,32,96]{3,2,1,0:T(8,128)S(1)} fusion(bf16[288,96,1,1]{1,0,3,2:T(8,128)(2,1)S(1)} %bitcast.115, bf16[4,16,32,96]{3,2,1,0:T(8,128)(2,1)S(1)} %multiply_convert_fusion, bf16[2,16,32,96]{3,2,1,0:T(8,128)(2,1)S(1)} %collective-permute-done, bf16[4,16,32,96]{3,2,1,0:T(8,128)(2,1)S(1)} %get-tuple-element.30, ...), kind=kOutput, calls=%fused_computation.11 | convolution fusion | flops 117964800 | bytes 2217984 | tf_op jit(solution)/shard_map/fhwk,ko->fhwo/dot_general | solution.py:49
  37.8 1.2 %fusion.162 = f32[4,16,32,96]{3,2,1,0:T(8,128)S(1)} fusion(f32[4,16,32,96]{3,2,1,0:T(8,128)S(1)} %fusion.49, f32[4,16,32,96]{3,2,1,0:T(8,128)S(1)} %fusion.43, f32[4,16,32,96]{3,2,1,0:T(8,128)S(1)} %fusion.37, f32[4,16,32,96]{3,2,1,0:T(8,128)S(1)} %fusion.8, f32[4,16,32,96]{3,2,1,0:T(8,128)S(1)} %fusion.29, f32[4,16,32,96]{3,2,1,0:T(8,128)S(1)} %fusion.23, ...), kind=kOutput, calls=%fused_computation.130 | convolution fusion | flops 118161408 | bytes 7526400 | tf_op jit(solution)/shard_map/fhwk,ko->fhwo/dot_general | solution.py:49
  39.0 0.9 %fusion.171 = bf16[4,16,32,96]{3,2,1,0:T(8,128)(2,1)S(1)} fusion(f32[4,16,32,96]{3,2,1,0:T(8,128)S(1)} %fusion.162, bf16[288,96,1,1]{1,0,3,2:T(8,128)(2,1)S(1)} %bitcast.113, bf16[4,16,32,96]{3,2,1,0:T(8,128)(2,1)S(1)} %get-tuple-element.40, bf16[4,16,32,96]{3,2,1,0:T(8,128)(2,1)S(1)} %get-tuple-element.47, ...), kind=kOutput, calls=%fused_computation.135 | convolution fusion | flops 117374976 | bytes 2414976 | tf_op jit(solution)/shard_map/fhwk,ko->fhwo/dot_general | solution.py:49
  40.0 0.0 copy-start.1
  40.0 0.3 fusion.184
  40.4 0.4 fusion.191
  40.8 2.1 %collective-permute-start.3 = (bf16[2,16,32,96]{3,2,1,0:T(8,128)(2,1)S(1)}, bf16[2,16,32,96]{3,2,1,0:T(8,128)(2,1)S(1)}, u32[]{:S(2)}, u32[]{:S(2)}) collective-permute-start(bf16[2,16,32,96]{3,2,1,0:T(8,128)(2,1)S(1)} %slice.441), channel_id=1, source_target_pairs={{0,16},{16,32},{32,48},{48,64},{64,80},{80,96},{96,112},{112,128},... | collective-permute-start | bytes 589832 | tf_op jit(solution)/shard_map/ppermute | solution.py:10
  43.0 9.2 %collective-permute-done.3 = bf16[2,16,32,96]{3,2,1,0:T(8,128)(2,1)S(1)} collective-permute-done((bf16[2,16,32,96]{3,2,1,0:T(8,128)(2,1)S(1)}, bf16[2,16,32,96]{3,2,1,0:T(8,128)(2,1)S(1)}, u32[]{:S(2)}, u32[]{:S(2)}) %collective-permute-start.3) | collective-permute-done | bytes 196640 | tf_op jit(solution)/shard_map/ppermute | solution.py:10
  52.2 2.0 %collective-permute-start.4 = (bf16[6,1,32,96]{3,2,1,0:T(8,128)(2,1)S(1)}, bf16[6,1,32,96]{3,2,1,0:T(8,128)(2,1)S(1)}, u32[]{:S(2)}, u32[]{:S(2)}) collective-permute-start(bf16[6,1,32,96]{3,2,1,0:T(8,128)(2,1)S(1)} %get-tuple-element.55), channel_id=1, source_target_pairs={{0,1},{1,2},{2,3},{3,4},{4,5},{5,6},{6,7},{7,8},{8,9},{9,10},{10,1... | collective-permute-start | bytes 110600 | tf_op jit(solution)/shard_map/ppermute | solution.py:21
  54.3 3.8 %collective-permute-start.5 = (bf16[6,1,32,96]{3,2,1,0:T(8,128)(2,1)S(1)}, bf16[6,1,32,96]{3,2,1,0:T(8,128)(2,1)S(1)}, u32[]{:S(2)}, u32[]{:S(2)}) collective-permute-start(bf16[6,1,32,96]{3,2,1,0:T(8,128)(2,1)S(1)} %get-tuple-element.56), channel_id=1, source_target_pairs={{1,0},{2,1},{3,2},{4,3},{5,4},{6,5},{7,6},{8,7},{9,8},{10,9},{11,1... | collective-permute-start | bytes 110600 | tf_op jit(solution)/shard_map/ppermute | solution.py:23
  58.1 0.1 fusion.192
  58.2 0.0 collective-permute-done.4
  58.2 4.1 %collective-permute-done.5 = bf16[6,1,32,96]{3,2,1,0:T(8,128)(2,1)S(1)} collective-permute-done((bf16[6,1,32,96]{3,2,1,0:T(8,128)(2,1)S(1)}, bf16[6,1,32,96]{3,2,1,0:T(8,128)(2,1)S(1)}, u32[]{:S(2)}, u32[]{:S(2)}) %collective-permute-start.5) | collective-permute-done | bytes 36896 | tf_op jit(solution)/shard_map/ppermute | solution.py:23
  62.3 0.5 select_maximum_fusion
  62.8 2.8 %fusion.212 = (bf16[4,16,32,96]{3,2,1,0:T(8,128)(2,1)S(1)}, bf16[4,16,32,96]{3,2,1,0:T(8,128)(2,1)S(1)}, bf16[4,16,32,96]{3,2,1,0:T(8,128)(2,1)S(1)}, bf16[4,16,...) fusion(bf16[6,18,34,96]{3,2,1,0:T(8,128)(2,1)S(1)} %select_maxi, ...), kind=kLoop, calls=%fused_computation.192 | loop fusion | bytes 14155776 | tf_op jit(solution)/shard_map/slice | solution.py:46
  65.6 0.2 pad_maximum_fusion.3
  65.8 0.2 fusion.214
  66.1 0.2 fusion.215
  66.3 0.9 %fusion.99 = f32[4,16,32,96]{3,2,1,0:T(8,128)S(1)} fusion(bf16[288,96,1,1]{1,0,3,2:T(8,128)(2,1)S(1)} %bitcast.126, bf16[4,16,32,96]{3,2,1,0:T(8,128)(2,1)S(1)} %get-tuple-element.6, bf16[4,16,32,96]{3,2,1,0:T(8,128)(2,1)S(1)} %fusion.191, bf16[4,16,32,96]{3,2,1,0:T(8,128)(2,1)S(1)} %get-tuple-element.7), kind=kOutput, calls=%fused_computation.101 | convolution fusion | flops 116785152 | bytes 2021376 | tf_op jit(solution)/shard_map/fhwk,ko->fhwo/dot_general | solution.py:49
  67.2 0.9 %fusion.67 = f32[4,16,32,96]{3,2,1,0:T(8,128)S(1)} fusion(bf16[288,96,1,1]{1,0,3,2:T(8,128)(2,1)S(1)} %bitcast.124, bf16[4,16,32,96]{3,2,1,0:T(8,128)(2,1)S(1)} %get-tuple-element.18, bf16[4,16,32,96]{3,2,1,0:T(8,128)(2,1)S(1)} %fusion.192, bf16[4,16,32,96]{3,2,1,0:T(8,128)(2,1)S(1)} %get-tuple-element.19), kind=kOutput, calls=%fused_computation.69 | convolution fusion | flops 116785152 | bytes 2021376 | tf_op jit(solution)/shard_map/fhwk,ko->fhwo/dot_general | solution.py:49
  68.2 0.9 %fusion.73 = f32[4,16,32,96]{3,2,1,0:T(8,128)S(1)} fusion(bf16[288,96,1,1]{1,0,3,2:T(8,128)(2,1)S(1)} %bitcast.122, bf16[4,16,32,96]{3,2,1,0:T(8,128)(2,1)S(1)} %get-tuple-element.16, bf16[4,16,32,96]{3,2,1,0:T(8,128)(2,1)S(1)} %get-tuple-element.43, bf16[4,16,32,96]{3,2,1,0:T(8,128)(2,1)S(1)} %get-tuple-element.17), kind=kOutput, calls=%fused_computation.75 | convolution fusion | flops 116785152 | bytes 2021376 | tf_op jit(solution)/shard_map/fhwk,ko->fhwo/dot_general | solution.py:49
  69.1 0.9 %fusion.79 = f32[4,16,32,96]{3,2,1,0:T(8,128)S(1)} fusion(bf16[288,96,1,1]{1,0,3,2:T(8,128)(2,1)S(1)} %bitcast.120, bf16[4,16,32,96]{3,2,1,0:T(8,128)(2,1)S(1)} %get-tuple-element.14, bf16[4,16,32,96]{3,2,1,0:T(8,128)(2,1)S(1)} %get-tuple-element.46, bf16[4,16,32,96]{3,2,1,0:T(8,128)(2,1)S(1)} %get-tuple-element.15), kind=kOutput, calls=%fused_computation.81 | convolution fusion | flops 116785152 | bytes 2021376 | tf_op jit(solution)/shard_map/fhwk,ko->fhwo/dot_general | solution.py:49
  70.1 0.9 %fusion.87 = f32[4,16,32,96]{3,2,1,0:T(8,128)S(1)} fusion(bf16[288,96,1,1]{1,0,3,2:T(8,128)(2,1)S(1)} %bitcast.118, bf16[4,16,32,96]{3,2,1,0:T(8,128)(2,1)S(1)} %get-tuple-element.10, bf16[4,16,32,96]{3,2,1,0:T(8,128)(2,1)S(1)} %get-tuple-element.42, bf16[4,16,32,96]{3,2,1,0:T(8,128)(2,1)S(1)} %get-tuple-element.11), kind=kOutput, calls=%fused_computation.89 | convolution fusion | flops 116785152 | bytes 2021376 | tf_op jit(solution)/shard_map/fhwk,ko->fhwo/dot_general | solution.py:49
  71.0 0.9 %fusion.93 = f32[4,16,32,96]{3,2,1,0:T(8,128)S(1)} fusion(bf16[288,96,1,1]{1,0,3,2:T(8,128)(2,1)S(1)} %bitcast.116, bf16[4,16,32,96]{3,2,1,0:T(8,128)(2,1)S(1)} %get-tuple-element.8, bf16[4,16,32,96]{3,2,1,0:T(8,128)(2,1)S(1)} %get-tuple-element.45, bf16[4,16,32,96]{3,2,1,0:T(8,128)(2,1)S(1)} %get-tuple-element.9), kind=kOutput, calls=%fused_computation.95 | convolution fusion | flops 116785152 | bytes 2021376 | tf_op jit(solution)/shard_map/fhwk,ko->fhwo/dot_general | solution.py:49
  71.9 0.9 %fusion.3 = f32[4,16,32,96]{3,2,1,0:T(8,128)S(1)} fusion(bf16[288,96,1,1]{1,0,3,2:T(8,128)(2,1)S(1)} %bitcast.114, bf16[4,16,32,96]{3,2,1,0:T(8,128)(2,1)S(1)} %fusion.191, bf16[2,16,32,96]{3,2,1,0:T(8,128)(2,1)S(1)} %collective-permute-done.3, bf16[4,16,32,96]{3,2,1,0:T(8,128)(2,1)S(1)} %get-tuple-element.12, bf16[4,16,32,96]{3,2,1,0:T(8,128)(2,1)S(1)} %get-tuple-element.13), kind=kOutput, calls=%fused_computation.6 | convolution fusion | flops 117964800 | bytes 2217984 | tf_op jit(solution)/shard_map/fhwk,ko->fhwo/dot_general | solution.py:49
  72.9 1.1 %fusion.165 = f32[4,16,32,96]{3,2,1,0:T(8,128)S(1)} fusion(f32[4,16,32,96]{3,2,1,0:T(8,128)S(1)} %fusion.99, f32[4,16,32,96]{3,2,1,0:T(8,128)S(1)} %fusion.93, f32[4,16,32,96]{3,2,1,0:T(8,128)S(1)} %fusion.87, f32[4,16,32,96]{3,2,1,0:T(8,128)S(1)} %fusion.3, f32[4,16,32,96]{3,2,1,0:T(8,128)S(1)} %fusion.79, f32[4,16,32,96]{3,2,1,0:T(8,128)S(1)} %fusion.73, ...), kind=kOutput, calls=%fused_computation.131 | convolution fusion | flops 118161408 | bytes 7526400 | tf_op jit(solution)/shard_map/fhwk,ko->fhwo/dot_general | solution.py:49
  74.0 1.0 %fusion.168 = bf16[4,16,32,96]{3,2,1,0:T(8,128)(2,1)S(1)} fusion(f32[4,16,32,96]{3,2,1,0:T(8,128)S(1)} %reshape.27, f32[4,16,32,96]{3,2,1,0:T(8,128)S(1)} %fusion.165, bf16[288,96,1,1]{1,0,3,2:T(8,128)(2,1)S(1)} %bitcast.112, bf16[4,16,32,96]{3,2,1,0:T(8,128)(2,1)S(1)} %get-tuple-element.22, bf16[4,16,32,96]{3,2,1,0:T(8,128)(2,1)S(1)} %get-tuple-element.41, ...), kind=kOutput, calls=%fused_computation.134 | convolution fusion | flops 117571584 | bytes 3201408 | tf_op jit(solution)/shard_map/fhwk,ko->fhwo/dot_general | solution.py:49
  74.9 1.5 %reshape.26 = bf16[4,16,3072]{2,1,0:T(8,128)(2,1)} reshape(bf16[4,16,32,96]{3,2,1,0:T(8,128)(2,1)S(1)} %fusion.168) | data formatting | bytes 786432 | tf_op jit(solution)/shard_map/reshape | solution.py:73
  (19 shorter events, 0.2 us)
Async XLA Ops:
  0.0 1.8 %copy-start.2 = (f32[96]{0:T(128)S(1)}, f32[96]{0:T(128)}, u32[]{:S(2)}) copy-start(f32[96]{0:T(128)} %param.8) | copy-start | bytes 1156
  1.8 2.4 %copy-start = (bf16[3,3,3,96,96]{4,3,2,1,0:T(8,128)(2,1)S(1)}, bf16[3,3,3,96,96]{4,3,2,1,0:T(8,128)(2,1)}, u32[]{:S(2)}) copy-start(bf16[3,3,3,96,96]{4,3,2,1,0:T(8,128)(2,1)} %param.9) | copy-start | bytes 1492996
  2.3 11.8 %collective-permute-start = (bf16[2,16,32,96]{3,2,1,0:T(8,128)(2,1)S(1)}, bf16[2,16,32,96]{3,2,1,0:T(8,128)(2,1)S(1)}, u32[]{:S(2)}, u32[]{:S(2)}) collective-permute-start(bf16[2,16,32,96]{3,2,1,0:T(8,128)(2,1)S(1)} %slice.414), channel_id=1, source_target_pairs={{0,16},{16,32},{32,48},{48,64},{64,80},{80,96},{96,112},{112,128},... | collective-permute-start | bytes 589832 | tf_op jit(solution)/shard_map/ppermute | solution.py:10
  14.1 6.8 %collective-permute-start.1 = (bf16[6,1,32,96]{3,2,1,0:T(8,128)(2,1)S(1)}, bf16[6,1,32,96]{3,2,1,0:T(8,128)(2,1)S(1)}, u32[]{:S(2)}, u32[]{:S(2)}) collective-permute-start(bf16[6,1,32,96]{3,2,1,0:T(8,128)(2,1)S(1)} %get-tuple-element.59), channel_id=1, source_target_pairs={{0,1},{1,2},{2,3},{3,4},{4,5},{5,6},{6,7},{7,8},{8,9},{9,10},{10,1... | collective-permute-start | bytes 110600 | tf_op jit(solution)/shard_map/ppermute | solution.py:21
  18.9 8.1 %collective-permute-start.2 = (bf16[6,1,32,96]{3,2,1,0:T(8,128)(2,1)S(1)}, bf16[6,1,32,96]{3,2,1,0:T(8,128)(2,1)S(1)}, u32[]{:S(2)}, u32[]{:S(2)}) collective-permute-start(bf16[6,1,32,96]{3,2,1,0:T(8,128)(2,1)S(1)} %get-tuple-element.60), channel_id=1, source_target_pairs={{1,0},{2,1},{3,2},{4,3},{5,4},{6,5},{7,6},{8,7},{9,8},{10,9},{11,1... | collective-permute-start | bytes 110600 | tf_op jit(solution)/shard_map/ppermute | solution.py:23
  37.8 1.3 %copy-start.4 = (f32[96]{0:T(128)S(1)}, f32[96]{0:T(128)}, u32[]{:S(2)}) copy-start(f32[96]{0:T(128)} %param.10) | copy-start | bytes 1156
  39.0 1.3 %copy-start.3 = (f32[96]{0:T(128)S(1)}, f32[96]{0:T(128)}, u32[]{:S(2)}) copy-start(f32[96]{0:T(128)} %param.11) | copy-start | bytes 1156
  40.0 2.9 %copy-start.1 = (bf16[3,3,3,96,96]{4,3,2,1,0:T(8,128)(2,1)S(1)}, bf16[3,3,3,96,96]{4,3,2,1,0:T(8,128)(2,1)}, u32[]{:S(2)}) copy-start(bf16[3,3,3,96,96]{4,3,2,1,0:T(8,128)(2,1)} %param.12) | copy-start | bytes 1492996
  40.8 11.4 %collective-permute-start.3 = (bf16[2,16,32,96]{3,2,1,0:T(8,128)(2,1)S(1)}, bf16[2,16,32,96]{3,2,1,0:T(8,128)(2,1)S(1)}, u32[]{:S(2)}, u32[]{:S(2)}) collective-permute-start(bf16[2,16,32,96]{3,2,1,0:T(8,128)(2,1)S(1)} %slice.441), channel_id=1, source_target_pairs={{0,16},{16,32},{32,48},{48,64},{64,80},{80,96},{96,112},{112,128},... | collective-permute-start | bytes 589832 | tf_op jit(solution)/shard_map/ppermute | solution.py:10
  52.2 6.0 %collective-permute-start.4 = (bf16[6,1,32,96]{3,2,1,0:T(8,128)(2,1)S(1)}, bf16[6,1,32,96]{3,2,1,0:T(8,128)(2,1)S(1)}, u32[]{:S(2)}, u32[]{:S(2)}) collective-permute-start(bf16[6,1,32,96]{3,2,1,0:T(8,128)(2,1)S(1)} %get-tuple-element.55), channel_id=1, source_target_pairs={{0,1},{1,2},{2,3},{3,4},{4,5},{5,6},{6,7},{7,8},{8,9},{9,10},{10,1... | collective-permute-start | bytes 110600 | tf_op jit(solution)/shard_map/ppermute | solution.py:21
  54.3 8.1 %collective-permute-start.5 = (bf16[6,1,32,96]{3,2,1,0:T(8,128)(2,1)S(1)}, bf16[6,1,32,96]{3,2,1,0:T(8,128)(2,1)S(1)}, u32[]{:S(2)}, u32[]{:S(2)}) collective-permute-start(bf16[6,1,32,96]{3,2,1,0:T(8,128)(2,1)S(1)} %get-tuple-element.56), channel_id=1, source_target_pairs={{1,0},{2,1},{3,2},{4,3},{5,4},{6,5},{7,6},{8,7},{9,8},{10,9},{11,1... | collective-permute-start | bytes 110600 | tf_op jit(solution)/shard_map/ppermute | solution.py:23
  72.9 1.1 %copy-start.5 = (f32[96]{0:T(128)S(1)}, f32[96]{0:T(128)}, u32[]{:S(2)}) copy-start(f32[96]{0:T(128)} %param.13) | copy-start | bytes 1156
where the time goes:
time: 76.6 us; the launch traced here: 76.4 us
  waiting for transfers between devices  29.3 us (38%)
  matrix products  17.2 us (22%)
  starting transfers between devices  16.6 us (22%)
  local copies, waits for them, and re-layouts  9.83 us (13%)
  other arithmetic  3.11 us (4%)
    ppermute x2, waiting for transfers between devices, shifted(): return lax.ppermute(value, axis, pairs)  19.1 us
    dot_general x18, matrix products, conv_local(): jnp.einsum('fhwk,ko->fhwo', stacked, kernel, preferred_element_type=jnp.f...  17.2 us
    ppermute x2, waiting for transfers between devices, with_halo(): lax.ppermute(head, axis, [((i + 1) % count, i) for i in range(ends)])  10.2 us
    ppermute x2, starting transfers between devices, with_halo(): lax.ppermute(tail, axis, [(i, (i + 1) % count) for i in range(ends)])  6.81 us
    ppermute x2, starting transfers between devices, with_halo(): lax.ppermute(head, axis, [((i + 1) % count, i) for i in range(ends)])  5.74 us
    slice x2, local copies, waits for them, and re-layouts, conv_local(): slab[:, :, 0:width]  5.55 us
    ppermute x2, starting transfers between devices, shifted(): return lax.ppermute(value, axis, pairs)  4.02 us
  transfers between devices with their start and end apart: 6, of which 4 were waited for; matrix products, arithmetic and copies ran while one was open for 0% of the time, Pallas kernels for 0%

commit v1 on v0

v1 whole, which is shorter than its diff:
```python
import jax
import jax.numpy as jnp
from jax import lax
from jax.experimental import pallas as pl
from jax.experimental.pallas import tpu as pltpu
from jax.sharding import PartitionSpec as P

C = 96
GROUP = 768
PAD = 128
LANES = 3072
WIDE = LANES + 2 * PAD
STARTS = (-128, 0, 384)
DEPTHS = (512, 768, 512)
HALVES = (
    ((96, (32, 0), (128, 96)), (64, (128, 96), (224, 64))),
    ((32, (96, 64), (192, 32)), (96, (288, 0), (384, 96))),
    ((64, (0, 96), (96, 64)), (32, (96, 64), (192, 32))),
)
BF = jnp.bfloat16
F32 = jnp.float32


def edges_kernel(x_ref, e0_ref, e1_ref):
    even = lax.rem(lax.axis_index("rows"), 2) == 0
    top, bot = [], []
    for row in range(2):
        for f in range(4):
            top.append(x_ref[f, 0:8, :].astype(F32)[row : row + 1])
    for row in range(2):
        for f in range(4):
            bot.append(x_ref[f, 8:16, :].astype(F32)[6 + row : 7 + row])
    top = jnp.concatenate(top, axis=0)
    bot = jnp.concatenate(bot, axis=0)
    e0_ref[...] = jnp.where(even, bot, top).astype(BF)
    e1_ref[...] = jnp.where(even, top, bot).astype(BF)


def band_kernel(w_ref, o0_ref, o1_ref, o2_ref):
    src = lax.broadcasted_iota(jnp.int32, (C, 256), 0)
    dst = lax.broadcasted_iota(jnp.int32, (C, 256), 1)

    def place(low, high):
        lane = lax.rem(dst, 128)
        turn = jnp.where(dst < 128, low, high)
        return jnp.where(lax.rem(src + turn, 128) == lane, 1.0, 0.0).astype(BF)

    first, second = place(0, 32), place(64, 96)
    outs = (o0_ref, o1_ref, o2_ref)

    def tap(k, carry):
        block = w_ref[pl.ds(3 * k, 3)].reshape(3 * C, C)
        a = jnp.dot(block, first, preferred_element_type=F32).astype(BF)
        b = jnp.dot(block, second, preferred_element_type=F32).astype(BF)
        turned = {0: a[:, :128], 32: a[:, 128:], 64: b[:, :128], 96: b[:, 128:]}
        for p in range(3):
            for half in range(2):
                edge, left, right = HALVES[p][half]

                def at(spot):
                    row, turn = spot
                    parts = [turned[turn]]
                    if row:
                        parts.insert(0, jnp.zeros((row, 128), BF))
                    rest = DEPTHS[p] - row - 3 * C
                    if rest:
                        parts.append(jnp.zeros((rest, 128), BF))
                    return jnp.concatenate(parts, axis=0)

                lane = lax.broadcasted_iota(jnp.int32, (DEPTHS[p], 128), 1)
                outs[p][k, :, 128 * half : 128 * half + 128] = jnp.where(lane < edge, at(left), at(right))
        return carry

    lax.fori_loop(0, 9, tap, 0)


def main_kernel(
    x_ref, prev_ref, h0_ref, h1_ref, c_ref, par_ref,
    u0, u1, u2, v0, v1, v2, out_ref,
    s1, a1, e, et, hid, hide, s2, a2,
):
    tm = lax.axis_index("tm")
    rows = lax.axis_index("rows")
    even = lax.rem(rows, 2) == 0
    lane = lax.broadcasted_iota(jnp.int32, (GROUP, 128), 0)
    col = lax.broadcasted_iota(jnp.int32, (GROUP, 128), 1)
    gather = jnp.where((lane >= col * C) & (lane < col * C + C), 1.0, 0.0).astype(BF)
    lane = lax.broadcasted_iota(jnp.int32, (256, GROUP), 1)
    col = lax.rem(lax.broadcasted_iota(jnp.int32, (256, GROUP), 0), 128)
    spread = jnp.where((lane >= col * C) & (lane < col * C + C), 1.0, 0.0).astype(BF)

    def act(v, gain):
        total = jnp.dot((v * v).astype(BF), gather, preferred_element_type=F32)
        r = lax.rsqrt(total * (1.0 / C) + 1e-06)
        high = r.astype(BF)
        low = (r - high.astype(F32)).astype(BF)
        wide = jnp.dot(jnp.concatenate([high, low], axis=1), spread, preferred_element_type=F32)
        half = v * wide * gain
        return half + half * jnp.tanh(half)

    def zero_sides(ref, index):
        shape = ref.shape[len(index) : -1]
        ref[index + (Ellipsis, pl.ds(0, PAD))] = jnp.zeros(shape + (PAD,), BF)
        ref[index + (Ellipsis, pl.ds(PAD + LANES, PAD))] = jnp.zeros(shape + (PAD,), BF)

    zero_sides(a1, ())
    zero_sides(et, ())
    zero_sides(a2, ())

    gain1 = par_ref[0:1, :]
    bias1 = par_ref[1:2, :]
    gain2 = par_ref[2:3, :]
    bias2 = par_ref[3:4, :]
    older = tm > 0

    for g in range(4):
        cut = pl.ds(GROUP * g, GROUP)
        h0, h1 = h0_ref[:, cut].astype(F32), h1_ref[:, cut].astype(F32)
        c0, c1 = c_ref[0:8, cut].astype(F32), c_ref[8:16, cut].astype(F32)
        up = jnp.where(rows > 0, jnp.where(even, h1, h0), 0.0)
        down = jnp.where(rows < 15, jnp.where(even, h0, h1), 0.0)
        up_old = jnp.where((rows > 0) & older, jnp.where(even, c1, c0), 0.0)
        down_old = jnp.where((rows < 15) & older, jnp.where(even, c0, c1), 0.0)
        both = act(jnp.concatenate([up_old, up, down_old, down], axis=0), gain1)
        e[0, 0:8, cut] = jnp.concatenate([both[0:4], both[8:12]], axis=0)
        e[1, 0:8, cut] = jnp.concatenate([both[4:8], both[12:16]], axis=0)
        e[4, 0:8, cut] = jnp.concatenate([both[16:20], both[24:28]], axis=0)
        e[5, 0:8, cut] = jnp.concatenate([both[20:24], both[28:32]], axis=0)

    for f in range(8):
        for g in range(4):
            cut = pl.ds(GROUP * g, GROUP)
            if f < 4:
                v = jnp.where(older, prev_ref[f, :, cut].astype(F32), 0.0)
            else:
                v = x_ref[f - 4, :, cut].astype(F32)
            s1[f, 8:24, cut] = act(v, gain1)
    for f in range(8):
        s1[f, 7:8, :] = e[1, f : f + 1, :]
        s1[f, 24:25, :] = e[4, f : f + 1, :]
        e[2, f : f + 1, :] = s1[f, 8:9, :]
        e[3, f : f + 1, :] = s1[f, 23:24, :]
    inner = pl.ds(PAD, LANES)
    for f in range(8):
        for kh in range(3):
            a1[kh, f, :, inner] = s1[f, 7 + kh : 23 + kh, :].astype(BF)
    for kt in range(3):
        for kh in range(3):
            et[kt, kh, :, inner] = jnp.concatenate(
                [e[kh, kt : kt + 8, :], e[3 + kh, kt : kt + 8, :]], axis=0
            ).astype(BF)

    for p, w in enumerate((u0, u1, u2)):
        depth = DEPTHS[p]
        taps = []
        for kt in range(3):
            for kh in range(3):
                parts = []
                for g in range(4):
                    cut = pl.ds(PAD + GROUP * g + STARTS[p], depth)
                    parts.append(a1[kh, kt : kt + 6, :, cut].reshape(96, depth))
                for g in range(4):
                    cut = pl.ds(PAD + GROUP * g + STARTS[p], depth)
                    parts.append(et[kt, kh, :, cut])
                taps.append(jnp.concatenate(parts, axis=0))
        total = jnp.dot(
            jnp.concatenate(taps, axis=1), w[...].reshape(9 * depth, 256), preferred_element_type=F32
        )
        total = (total + bias1[:, 256 * p : 256 * p + 256]).astype(BF)
        for g in range(4):
            cut = pl.ds(GROUP * g + 256 * p, 256)
            hid[:, :, cut] = total[96 * g : 96 * g + 96].reshape(6, 16, 256)
            hide[:, cut] = total[384 + 16 * g : 400 + 16 * g]

    spot = lax.broadcasted_iota(jnp.int32, (16, GROUP), 0)
    frame = lax.rem(spot, 8)
    keep = ((spot >= 8) | (rows > 0)) & ((spot < 8) | (rows < 15)) & ((frame >= 2) | older)
    for f in range(6):
        for g in range(4):
            cut = pl.ds(GROUP * g, GROUP)
            v = act(hid[f, :, cut].astype(F32), gain2)
            if f < 2:
                v = jnp.where(older, v, 0.0)
            s2[f, 8:24, cut] = v
    for g in range(4):
        cut = pl.ds(GROUP * g, GROUP)
        e[0, :, cut] = jnp.where(keep, act(hide[:, cut].astype(F32), gain2), 0.0)
    for f in range(6):
        s2[f, 7:8, :] = e[0, f : f + 1, :]
        s2[f, 24:25, :] = e[0, 8 + f : 9 + f, :]
    for f in range(6):
        for kh in range(3):
            a2[kh, f, :, inner] = s2[f, 7 + kh : 23 + kh, :].astype(BF)

    for p, w in enumerate((v0, v1, v2)):
        depth = DEPTHS[p]
        taps = []
        for kt in range(3):
            for kh in range(3):
                parts = []
                for g in range(4):
                    cut = pl.ds(PAD + GROUP * g + STARTS[p], depth)
                    parts.append(a2[kh, kt : kt + 4, :, cut].reshape(64, depth))
                taps.append(jnp.concatenate(parts, axis=0))
        total = jnp.dot(
            jnp.concatenate(taps, axis=1), w[...].reshape(9 * depth, 256), preferred_element_type=F32
        )
        total = total + bias2[:, 256 * p : 256 * p + 256]
        for g in range(4):
            cut = pl.ds(GROUP * g + 256 * p, 256)
            out_ref[:, :, cut] = (
                x_ref[:, :, cut].astype(F32) + total[64 * g : 64 * g + 64].reshape(4, 16, 256)
            ).astype(BF)


def vmem():
    return pl.BlockSpec(memory_space=pltpu.VMEM)


def make_pairs(tms, rws):
    def flat(move):
        pairs = []
        for t in range(tms):
            for r in range(rws):
                to_t, to_r = move(t, r)
                pairs.append((t * rws + r, to_t * rws + to_r))
        return pairs

    def odd(t, r):
        if r in (0, rws - 1):
            return t ^ 1, r
        return t, (r + 1 if r % 2 else r - 1)

    return (
        flat(lambda t, r: (t, r ^ 1)),
        flat(odd),
        flat(lambda t, r: ((t + 1) % tms, r)),
    )


def solution(mesh):
    even_swap, odd_swap, later = make_pairs(mesh.shape["tm"], mesh.shape["rows"])
    axes = ("tm", "rows")

    def body(frames, gain_one, weight_one, bias_one, gain_two, weight_two, bias_two):
        prev = lax.ppermute(frames, axes, later)
        edge = jax.ShapeDtypeStruct((8, LANES), BF)
        e0, e1 = pl.pallas_call(
            edges_kernel, out_shape=(edge, edge), in_specs=[vmem()], out_specs=(vmem(), vmem()), name="edges"
        )(frames)
        h0 = lax.ppermute(e0, axes, even_swap)
        h1 = lax.ppermute(e1, axes, odd_swap)
        corners = lax.ppermute(jnp.concatenate([h0, h1], axis=0), axes, later)
        params = jnp.stack([0.5 * gain_one, bias_one, 0.5 * gain_two, bias_two])
        params = jnp.tile(params, (1, GROUP // C))

        def bands(w):
            return pl.pallas_call(
                band_kernel,
                out_shape=tuple(pltpu.VMEM((9, d, 256), BF) for d in DEPTHS),
                in_specs=[vmem()],
                out_specs=(vmem(),) * 3,
                compiler_params=pltpu.CompilerParams(vmem_limit_bytes=8 << 20),
                name="bands",
            )(w.reshape(27, C, C))

        u = bands(weight_one)
        v = bands(weight_two)
        return pl.pallas_call(
            main_kernel,
            out_shape=jax.ShapeDtypeStruct((4, 16, LANES), BF),
            in_specs=[vmem()] * 12,
            out_specs=vmem(),
            scratch_shapes=[
                pltpu.VMEM((8, 32, LANES), F32),
                pltpu.VMEM((3, 8, 16, WIDE), BF),
                pltpu.VMEM((6, 16, LANES), F32),
                pltpu.VMEM((3, 3, 16, WIDE), BF),
                pltpu.VMEM((6, 16, LANES), BF),
                pltpu.VMEM((16, LANES), BF),
                pltpu.VMEM((6, 32, LANES), F32),
                pltpu.VMEM((3, 6, 16, WIDE), BF),
            ],
            compiler_params=pltpu.CompilerParams(vmem_limit_bytes=40 << 20),
            name="block",
        )(frames, prev, h0, h1, corners, params, *u, *v)

    in_specs = (P("tm", "rows", None), P(), P(), P(), P(), P(), P())
    out_specs = P("tm", "rows", None)
    return jax.shard_map(body, mesh=mesh, in_specs=in_specs, out_specs=out_specs, check_vma=False)
```

time: 76.6 us -> 47.8 us (0.62)
  the two profiles are of different devices: /device:TPU:120 before, /device:TPU:103 now
where the time goes in v1:
time: 47.8 us; the launch traced here: 47.5 us
  Pallas kernels  28.5 us (60%)
  starting transfers between devices  9.77 us (20%)
  local copies, waits for them, and re-layouts  5 us (10%)
  waiting for transfers between devices  2.77 us (6%)
  other arithmetic  1.36 us (3%)
    pallas_call x1, Pallas kernels, body(): pl.pallas_call(main_kernel, out_shape=jax.ShapeDtypeStruct((4, 16, LANES)...  21.7 us
    ppermute x1, starting transfers between devices, body(): corners = lax.ppermute(jnp.concatenate([h0, h1], axis=0), axes, later)  5.37 us
    pallas_call x2, Pallas kernels, bands(): pl.pallas_call(band_kernel, out_shape=tuple((pltpu.VMEM((9, d, 256), BF)...  5 us
    unnamed x8, local copies, waits for them, and re-layouts  4.91 us
    ppermute x1, starting transfers between devices, body(): prev = lax.ppermute(frames, axes, later)  3.39 us
    ppermute x1, waiting for transfers between devices, body(): h0 = lax.ppermute(e0, axes, even_swap)  1.99 us
    pallas_call x1, Pallas kernels, body(): pl.pallas_call(edges_kernel, out_shape=(edge, edge), in_specs=[vmem()], o...  1.78 us
    another operation x2, other arithmetic, body(): params = jnp.stack([0.5 * gain_one, bias_one, 0.5 * gain_two, bias_two])  1.36 us
  transfers between devices with their start and end apart: 4, of which 2 were waited for; matrix products, arithmetic and copies ran while one was open for 3% of the time, Pallas kernels for 14%

profile of v1, /device:TPU:103, one launch (start us, length us, event | category | flops | bytes accessed | tf_op | source)
XLA Modules:
  0.0 47.5 jit_solution(3906083769896406719)
XLA Ops:
  0.0 3.4 %collective-permute-start = (bf16[4,16,3072]{2,1,0:T(8,128)(2,1)}, bf16[4,16,3072]{2,1,0:T(8,128)(2,1)S(1)}, u32[]{:S(2)}, u32[]{:S(2)}) collective-permute-start(bf16[4,16,3072]{2,1,0:T(8,128)(2,1)} %x_ref.3), channel_id=1, source_target_pairs={{0,16},{1,17},{2,18},{3,19},{4,20},{5,21},{6,22},{7,23},{8,24},{9,... | collective-permute-start | bytes 1179656 | tf_op jit(solution)/shard_map/ppermute | solution.py:246
  3.4 1.8 %edges.1 = (bf16[8,3072]{1,0:T(8,128)(2,1)}, bf16[8,3072]{1,0:T(8,128)(2,1)}) custom-call(bf16[4,16,3072]{2,1,0:T(8,128)(2,1)} %x_ref.3), custom_call_target="tpu_custom_call" | custom-call | tf_op jit(solution)/shard_map/edges/pallas_call | solution.py:248
  5.2 0.4 collective-permute-start.1
  5.6 0.6 %collective-permute-start.2 = (bf16[8,3072]{1,0:T(8,128)(2,1)}, bf16[8,3072]{1,0:T(8,128)(2,1)S(1)}, u32[]{:S(2)}, u32[]{:S(2)}) collective-permute-start(bf16[8,3072]{1,0:T(8,128)(2,1)} %get-tuple-element.14), channel_id=1, source_target_pairs={{0,16},{1,2},{2,1},{3,4},{4,3},{5,6},{6,5},{7,8},{8,7},{9,10},{10,... | collective-permute-start | bytes 147464 | tf_op jit(solution)/shard_map/ppermute | solution.py:252
  6.2 0.7 %multiply_bitcast_fusion = (f32[1,96]{1,0:T(1,128)S(1)}, f32[1,96]{1,0:T(1,128)S(1)}) fusion(f32[96]{0:T(128)} %param.11, f32[96]{0:T(128)} %param.8), kind=kLoop, calls=%fused_computation.2 | loop fusion | flops 192 | bytes 1536 | tf_op jit(solution)/shard_map/stack | solution.py:254
  6.9 2.0 %collective-permute-done.1.h0_ref = bf16[8,3072]{1,0:T(8,128)(2,1)S(1)} collective-permute-done((bf16[8,3072]{1,0:T(8,128)(2,1)}, bf16[8,3072]{1,0:T(8,128)(2,1)S(1)}, u32[]{:S(2)}, u32[]{:S(2)}) %collective-permute-start.1) | collective-permute-done | bytes 49184 | tf_op jit(solution)/shard_map/ppermute | solution.py:251
  8.9 0.8 %collective-permute-done.2.h1_ref = bf16[8,3072]{1,0:T(8,128)(2,1)S(1)} collective-permute-done((bf16[8,3072]{1,0:T(8,128)(2,1)}, bf16[8,3072]{1,0:T(8,128)(2,1)S(1)}, u32[]{:S(2)}, u32[]{:S(2)}) %collective-permute-start.2) | collective-permute-done | bytes 49184 | tf_op jit(solution)/shard_map/ppermute | solution.py:252
  9.6 5.4 %collective-permute-start.3 = (bf16[16,3072]{1,0:T(8,128)(2,1)S(1)}, bf16[16,3072]{1,0:T(8,128)(2,1)S(1)}, u32[]{:S(2)}, u32[]{:S(2)}) collective-permute-start(bf16[16,3072]{1,0:T(8,128)(2,1)S(1)} %pad_maximum_fusion), channel_id=1, source_target_pairs={{0,16},{1,17},{2,18},{3,19},{4,20},{5,21},{6,22},{7,23},{8,24},{9,... | collective-permute-start | bytes 294920 | tf_op jit(solution)/shard_map/ppermute | solution.py:253
  15.0 0.7 %pad_maximum_fusion.1 = f32[4,96]{1,0:T(4,128)S(1)} fusion(f32[1,96]{1,0:T(1,128)} %bitcast.10, f32[1,96]{1,0:T(1,128)S(1)} %get-tuple-element.21, f32[1,96]{1,0:T(1,128)} %bitcast.11, f32[1,96]{1,0:T(1,128)S(1)} %get-tuple-element.22), kind=kLoop, calls=%fused_computation.1 | loop fusion | flops 1152 | bytes 3072 | tf_op jit(solution)/shard_map/stack | solution.py:254
  15.7 0.1 tile.10.par_ref
  15.8 0.0 copy-start.2
  15.8 1.1 %copy-done.2 = bf16[3,3,3,96,96]{4,3,2,1,0:T(8,128)(2,1)S(1)} copy-done((bf16[3,3,3,96,96]{4,3,2,1,0:T(8,128)(2,1)S(1)}, bf16[3,3,3,96,96]{4,3,2,1,0:T(8,128)(2,1)}, u32[]{:S(2)}) %copy-start.2) | copy-done | bytes 497688
  16.9 2.4 %bands.2 = (bf16[9,512,256]{2,1,0:T(8,128)(2,1)S(1)}, bf16[9,768,256]{2,1,0:T(8,128)(2,1)S(1)}, bf16[9,512,256]{2,1,0:T(8,128)(2,1)S(1)}) custom-call(bf16[27,96,96]{2,1,0:T(8,128)(2,1)S(1)} %bitcast.8), custom_call_target="tpu_custom_call" | custom-call | tf_op jit(solution)/shard_map/bands/pallas_call | solution.py:258
  19.3 0.0 copy-start.3
  19.3 1.1 %copy-done.3 = bf16[3,3,3,96,96]{4,3,2,1,0:T(8,128)(2,1)S(1)} copy-done((bf16[3,3,3,96,96]{4,3,2,1,0:T(8,128)(2,1)S(1)}, bf16[3,3,3,96,96]{4,3,2,1,0:T(8,128)(2,1)}, u32[]{:S(2)}) %copy-start.3) | copy-done | bytes 497688
  20.4 2.6 %bands.3 = (bf16[9,512,256]{2,1,0:T(8,128)(2,1)S(1)}, bf16[9,768,256]{2,1,0:T(8,128)(2,1)S(1)}, bf16[9,512,256]{2,1,0:T(8,128)(2,1)S(1)}) custom-call(bf16[27,96,96]{2,1,0:T(8,128)(2,1)S(1)} %bitcast.9), custom_call_target="tpu_custom_call" | custom-call | tf_op jit(solution)/shard_map/bands/pallas_call | solution.py:258
  23.0 0.0 copy-start
  23.0 1.7 %copy-done = bf16[9,768,256]{2,1,0:T(8,128)(2,1)} copy-done((bf16[9,768,256]{2,1,0:T(8,128)(2,1)}, bf16[9,768,256]{2,1,0:T(8,128)(2,1)S(1)}, u32[]{:S(2)}) %copy-start) | copy-done | bytes 3538968
  24.7 0.0 collective-permute-done.3.c_ref
  24.7 0.0 collective-permute-done.prev_ref
  24.7 0.0 copy-start.1
  24.7 1.0 %copy-done.1 = bf16[4,16,3072]{2,1,0:T(8,128)(2,1)S(1)} copy-done((bf16[4,16,3072]{2,1,0:T(8,128)(2,1)S(1)}, bf16[4,16,3072]{2,1,0:T(8,128)(2,1)}, u32[]{:S(2)}) %copy-start.1) | copy-done | bytes 393240
  25.7 21.7 %block.1 = bf16[4,16,3072]{2,1,0:T(8,128)(2,1)} custom-call(bf16[4,16,3072]{2,1,0:T(8,128)(2,1)S(1)} %copy-done.1, bf16[4,16,3072]{2,1,0:T(8,128)(2,1)S(1)} %collective-permute-done.prev_ref, bf16[8,3072]{1,0:T(8,128)(2,1)S(1)} %collective-permute-done.1.h0_ref, bf16[8,3072]{1,0:T(8,128)(2,1)S(1)} %collective-permute-done.2.h1_ref, ...), custom_call_target="tpu_custom_call" | custom-call | tf_op jit(solution)/shard_map/block/pallas_call | solution.py:269
  (2 shorter events, 0.0 us)
Async XLA Ops:
  0.0 24.7 %collective-permute-start = (bf16[4,16,3072]{2,1,0:T(8,128)(2,1)}, bf16[4,16,3072]{2,1,0:T(8,128)(2,1)S(1)}, u32[]{:S(2)}, u32[]{:S(2)}) collective-permute-start(bf16[4,16,3072]{2,1,0:T(8,128)(2,1)} %x_ref.3), channel_id=1, source_target_pairs={{0,16},{1,17},{2,18},{3,19},{4,20},{5,21},{6,22},{7,23},{8,24},{9,... | collective-permute-start | bytes 1179656 | tf_op jit(solution)/shard_map/ppermute | solution.py:246
  5.2 3.7 %collective-permute-start.1 = (bf16[8,3072]{1,0:T(8,128)(2,1)}, bf16[8,3072]{1,0:T(8,128)(2,1)S(1)}, u32[]{:S(2)}, u32[]{:S(2)}) collective-permute-start(bf16[8,3072]{1,0:T(8,128)(2,1)} %get-tuple-element.13), channel_id=1, source_target_pairs={{0,1},{1,0},{2,3},{3,2},{4,5},{5,4},{6,7},{7,6},{8,9},{9,8},{10,11... | collective-permute-start | bytes 147464 | tf_op jit(solution)/shard_map/ppermute | solution.py:251
  5.6 4.0 %collective-permute-start.2 = (bf16[8,3072]{1,0:T(8,128)(2,1)}, bf16[8,3072]{1,0:T(8,128)(2,1)S(1)}, u32[]{:S(2)}, u32[]{:S(2)}) collective-permute-start(bf16[8,3072]{1,0:T(8,128)(2,1)} %get-tuple-element.14), channel_id=1, source_target_pairs={{0,16},{1,2},{2,1},{3,4},{4,3},{5,6},{6,5},{7,8},{8,7},{9,10},{10,... | collective-permute-start | bytes 147464 | tf_op jit(solution)/shard_map/ppermute | solution.py:252
  9.6 15.1 %collective-permute-start.3 = (bf16[16,3072]{1,0:T(8,128)(2,1)S(1)}, bf16[16,3072]{1,0:T(8,128)(2,1)S(1)}, u32[]{:S(2)}, u32[]{:S(2)}) collective-permute-start(bf16[16,3072]{1,0:T(8,128)(2,1)S(1)} %pad_maximum_fusion), channel_id=1, source_target_pairs={{0,16},{1,17},{2,18},{3,19},{4,20},{5,21},{6,22},{7,23},{8,24},{9,... | collective-permute-start | bytes 294920 | tf_op jit(solution)/shard_map/ppermute | solution.py:253
  15.8 1.1 %copy-start.2 = (bf16[3,3,3,96,96]{4,3,2,1,0:T(8,128)(2,1)S(1)}, bf16[3,3,3,96,96]{4,3,2,1,0:T(8,128)(2,1)}, u32[]{:S(2)}) copy-start(bf16[3,3,3,96,96]{4,3,2,1,0:T(8,128)(2,1)} %param.9) | copy-start | bytes 1492996
  19.3 1.1 %copy-start.3 = (bf16[3,3,3,96,96]{4,3,2,1,0:T(8,128)(2,1)S(1)}, bf16[3,3,3,96,96]{4,3,2,1,0:T(8,128)(2,1)}, u32[]{:S(2)}) copy-start(bf16[3,3,3,96,96]{4,3,2,1,0:T(8,128)(2,1)} %param.12) | copy-start | bytes 1492996
  23.0 1.7 %copy-start = (bf16[9,768,256]{2,1,0:T(8,128)(2,1)}, bf16[9,768,256]{2,1,0:T(8,128)(2,1)S(1)}, u32[]{:S(2)}) copy-start(bf16[9,768,256]{2,1,0:T(8,128)(2,1)S(1)} %get-tuple-element.19.v1) | copy-start | bytes 10616836
  24.7 1.0 %copy-start.1 = (bf16[4,16,3072]{2,1,0:T(8,128)(2,1)S(1)}, bf16[4,16,3072]{2,1,0:T(8,128)(2,1)}, u32[]{:S(2)}) copy-start(bf16[4,16,3072]{2,1,0:T(8,128)(2,1)} %x_ref.3) | copy-start | bytes 1179652

commit v2 on v1

v2 whole, which is shorter than its diff:
```python
import jax
import jax.numpy as jnp
from jax import lax
from jax.experimental import pallas as pl
from jax.experimental.pallas import tpu as pltpu
from jax.sharding import PartitionSpec as P

C = 96
GROUP = 768
PAD = 128
LANES = 3072
WIDE = LANES + 2 * PAD
STARTS = (-128, 0, 384)
DEPTHS = (512, 768, 512)
HALVES = (
    ((96, (32, 0), (128, 96)), (64, (128, 96), (224, 64))),
    ((32, (96, 64), (192, 32)), (96, (288, 0), (384, 96))),
    ((64, (0, 96), (96, 64)), (32, (96, 64), (192, 32))),
)
BF = jnp.bfloat16
F32 = jnp.float32


def edges_kernel(x_ref, e0_ref, e1_ref):
    even = lax.rem(lax.axis_index("rows"), 2) == 0
    top, bot = [], []
    for row in range(2):
        for f in range(4):
            top.append(x_ref[f, 0:8, :].astype(F32)[row : row + 1])
    for row in range(2):
        for f in range(4):
            bot.append(x_ref[f, 8:16, :].astype(F32)[6 + row : 7 + row])
    top = jnp.concatenate(top, axis=0)
    bot = jnp.concatenate(bot, axis=0)
    e0_ref[...] = jnp.where(even, bot, top).astype(BF)
    e1_ref[...] = jnp.where(even, top, bot).astype(BF)


def band_kernel(
    w1_ref, w2_ref, p0, p1, p2, p3, o0, o1, o2, q0, q1, q2, par_ref, buf, small, sems, small_sems
):
    tiny = []
    for n, ref in enumerate((p0, p1, p2, p3)):
        tiny.append(pltpu.make_async_copy(ref, small.at[n], small_sems.at[n]))
        tiny[-1].start()
    copies = []
    for n, ref in enumerate((w1_ref, w2_ref)):
        for k in range(3):
            copies.append(pltpu.make_async_copy(ref.at[k], buf.at[n, k], sems.at[n, k]))
            copies[-1].start()
    src = lax.broadcasted_iota(jnp.int32, (C, 256), 0)
    dst = lax.broadcasted_iota(jnp.int32, (C, 256), 1)

    def place(low, high):
        lane = lax.rem(dst, 128)
        turn = jnp.where(dst < 128, low, high)
        return jnp.where(lax.rem(src + turn, 128) == lane, 1.0, 0.0).astype(BF)

    first, second = place(0, 32), place(64, 96)
    for n, outs in enumerate(((o0, o1, o2), (q0, q1, q2))):
        for kt in range(3):
            copies[3 * n + kt].wait()
            block = buf[n, kt].reshape(9 * C, C)
            a = jnp.dot(block, first, preferred_element_type=F32).astype(BF)
            b = jnp.dot(block, second, preferred_element_type=F32).astype(BF)
            for kh in range(3):
                part = slice(3 * C * kh, 3 * C * kh + 3 * C)
                turned = {0: a[part, :128], 32: a[part, 128:], 64: b[part, :128], 96: b[part, 128:]}
                for p in range(3):
                    for half in range(2):
                        edge, left, right = HALVES[p][half]

                        def at(spot):
                            row, turn = spot
                            parts = [turned[turn]]
                            if row:
                                parts.insert(0, jnp.zeros((row, 128), BF))
                            rest = DEPTHS[p] - row - 3 * C
                            if rest:
                                parts.append(jnp.zeros((rest, 128), BF))
                            return jnp.concatenate(parts, axis=0)

                        lane = lax.broadcasted_iota(jnp.int32, (DEPTHS[p], 128), 1)
                        outs[p][3 * kt + kh, :, 128 * half : 128 * half + 128] = jnp.where(
                            lane < edge, at(left), at(right)
                        )
    for copy in tiny:
        copy.wait()
    params = jnp.concatenate([0.5 * small[0], small[1], 0.5 * small[2], small[3]], axis=0)
    par_ref[...] = jnp.concatenate([params] * (GROUP // C), axis=1)


def bands(weight_one, weight_two, params):
    far = [weight_one.reshape(3, 9, C, C), weight_two.reshape(3, 9, C, C)] + [q.reshape(1, C) for q in params]
    far = [pltpu.with_memory_space_constraint(q, pltpu.HBM) for q in far]
    return pl.pallas_call(
        band_kernel,
        out_shape=tuple(pltpu.VMEM((9, d, 256), BF) for d in DEPTHS * 2) + (pltpu.VMEM((4, GROUP), F32),),
        in_specs=[pl.BlockSpec(memory_space=pltpu.HBM)] * 6,
        out_specs=(vmem(),) * 7,
        scratch_shapes=[
            pltpu.VMEM((2, 3, 9, C, C), BF),
            pltpu.VMEM((4, 1, C), F32),
            pltpu.SemaphoreType.DMA((2, 3)),
            pltpu.SemaphoreType.DMA((4,)),
        ],
        compiler_params=pltpu.CompilerParams(vmem_limit_bytes=8 << 20),
        cost_estimate=pl.CostEstimate(flops=4000000000, bytes_accessed=18000000, transcendentals=0),
        name="bands",
    )(*far)


def main_kernel(
    x_ref, prev_ref, h0_ref, h1_ref, c0_ref, c1_ref,
    u0, u1, u2, v0, v1, v2, par_ref, out_ref,
    square, scale, a1, e, et, hid, a2,
):
    tm = lax.axis_index("tm")
    rows = lax.axis_index("rows")
    even = lax.rem(rows, 2) == 0
    older = tm > 0
    lane = lax.broadcasted_iota(jnp.int32, (GROUP, 128), 0)
    col = lax.broadcasted_iota(jnp.int32, (GROUP, 128), 1)
    gather = jnp.where((lane >= col * C) & (lane < col * C + C), 1.0, 0.0).astype(BF)
    lane = lax.broadcasted_iota(jnp.int32, (256, GROUP), 1)
    col = lax.rem(lax.broadcasted_iota(jnp.int32, (256, GROUP), 0), 128)
    spread = jnp.where((lane >= col * C) & (lane < col * C + C), 1.0, 0.0).astype(BF)

    def norm(count):
        total = jnp.dot(square[0:count, :], gather, preferred_element_type=F32)
        r = lax.rsqrt(total * (1.0 / C) + 1e-06)
        high = r.astype(BF)
        low = (r - high.astype(F32)).astype(BF)
        scale[0:count, :] = jnp.dot(jnp.concatenate([high, low], axis=1), spread, preferred_element_type=F32)

    def act(v, where, gain):
        half = v.astype(F32) * scale[where, :] * gain
        return half + half * jnp.tanh(half)

    def zero_sides(ref):
        shape = ref.shape[:-1]
        ref[..., pl.ds(0, PAD)] = jnp.zeros(shape + (PAD,), BF)
        ref[..., pl.ds(PAD + LANES, PAD)] = jnp.zeros(shape + (PAD,), BF)

    zero_sides(a1)
    zero_sides(et)
    zero_sides(a2)

    gain1 = par_ref[0:1, :]
    bias1 = par_ref[1:2, :]
    gain2 = par_ref[2:3, :]
    bias2 = par_ref[3:4, :]

    def shifted(ref, f, g, v, above, below):
        cut = pl.ds(PAD + GROUP * g, GROUP)
        ref[0, f, :, cut] = jnp.concatenate([above, v[0:15]], axis=0).astype(BF)
        ref[1, f, :, cut] = v.astype(BF)
        ref[2, f, :, cut] = jnp.concatenate([v[1:16], below], axis=0).astype(BF)

    zero = jnp.zeros((), BF)
    halos = []
    for g in range(4):
        cut = pl.ds(GROUP * g, GROUP)
        h0, h1 = h0_ref[:, cut].astype(F32), h1_ref[:, cut].astype(F32)
        c0, c1 = c0_ref[:, cut].astype(F32), c1_ref[:, cut].astype(F32)
        up = jnp.where(rows > 0, jnp.where(even, h1, h0), 0.0)
        down = jnp.where(rows < 15, jnp.where(even, h0, h1), 0.0)
        up_old = jnp.where((rows > 0) & older, jnp.where(even, c1, c0), 0.0)
        down_old = jnp.where((rows < 15) & older, jnp.where(even, c0, c1), 0.0)
        halo = jnp.concatenate([up_old, up, down_old, down], axis=0).astype(BF)
        e[0, 0:8, cut] = up_old
        e[1, 0:8, cut] = up
        e[4, 0:8, cut] = down_old
        e[5, 0:8, cut] = down
        before = jnp.where(older, prev_ref[:, :, cut].reshape(64, GROUP), zero)
        own = x_ref[:, :, cut].reshape(64, GROUP)
        square[160 * g : 160 * g + 64, :] = before * before
        square[160 * g + 64 : 160 * g + 128, :] = own * own
        square[160 * g + 128 : 160 * g + 160, :] = halo * halo
    norm(640)
    for g in range(4):
        cut = pl.ds(GROUP * g, GROUP)
        at = 160 * g + 128
        up_old = act(e[0, 0:8, cut], pl.ds(at, 8), gain1)
        up = act(e[1, 0:8, cut], pl.ds(at + 8, 8), gain1)
        down_old = act(e[4, 0:8, cut], pl.ds(at + 16, 8), gain1)
        down = act(e[5, 0:8, cut], pl.ds(at + 24, 8), gain1)
        e[0, 0:8, cut] = jnp.concatenate([up_old[0:4], up[0:4]], axis=0)
        e[1, 0:8, cut] = jnp.concatenate([up_old[4:8], up[4:8]], axis=0)
        e[4, 0:8, cut] = jnp.concatenate([down_old[0:4], down[0:4]], axis=0)
        e[5, 0:8, cut] = jnp.concatenate([down_old[4:8], down[4:8]], axis=0)
        for f in range(8):
            if f < 4:
                v = jnp.where(older, prev_ref[f, :, cut], zero)
            else:
                v = x_ref[f - 4, :, cut]
            v = act(v, pl.ds(160 * g + 16 * f, 16), gain1)
            shifted(a1, f, g, v, e[1, f : f + 1, cut], e[4, f : f + 1, cut])
            e[2, f : f + 1, cut] = v[0:1]
            e[3, f : f + 1, cut] = v[15:16]
        for kt in range(3):
            for kh in range(3):
                et[kt, kh, :, pl.ds(PAD + GROUP * g, GROUP)] = jnp.concatenate(
                    [e[kh, kt : kt + 8, cut], e[3 + kh, kt : kt + 8, cut]], axis=0
                ).astype(BF)

    for p, w in enumerate((u0, u1, u2)):
        depth = DEPTHS[p]
        taps = []
        for kt in range(3):
            for kh in range(3):
                parts = []
                for g in range(4):
                    cut = pl.ds(PAD + GROUP * g + STARTS[p], depth)
                    parts.append(a1[kh, kt : kt + 6, :, cut].reshape(96, depth))
                    parts.append(et[kt, kh, :, cut])
                taps.append(jnp.concatenate(parts, axis=0))
        total = jnp.dot(
            jnp.concatenate(taps, axis=1), w[...].reshape(9 * depth, 256), preferred_element_type=F32
        )
        cut = pl.ds(256 * p, 256)
        total = (total + bias1[:, 256 * p : 256 * p + 256]).astype(BF)
        hid[:, cut] = total
        square[0:448, cut] = total * total

    norm(448)
    spot = lax.broadcasted_iota(jnp.int32, (16, GROUP), 0)
    frame = lax.rem(spot, 8)
    keep = ((spot >= 8) | (rows > 0)) & ((spot < 8) | (rows < 15)) & ((frame >= 2) | older)
    for g in range(4):
        cut = pl.ds(GROUP * g, GROUP)
        at = pl.ds(112 * g + 96, 16)
        e[0, :, cut] = jnp.where(keep, act(hid[at, :], at, gain2), 0.0)
        for f in range(6):
            at = pl.ds(112 * g + 16 * f, 16)
            v = act(hid[at, :], at, gain2)
            if f < 2:
                v = jnp.where(older, v, 0.0)
            shifted(a2, f, g, v, e[0, f : f + 1, cut], e[0, 8 + f : 9 + f, cut])

    for p, w in enumerate((v0, v1, v2)):
        depth = DEPTHS[p]
        taps = []
        for kt in range(3):
            for kh in range(3):
                parts = []
                for g in range(4):
                    cut = pl.ds(PAD + GROUP * g + STARTS[p], depth)
                    parts.append(a2[kh, kt : kt + 4, :, cut].reshape(64, depth))
                taps.append(jnp.concatenate(parts, axis=0))
        total = jnp.dot(
            jnp.concatenate(taps, axis=1), w[...].reshape(9 * depth, 256), preferred_element_type=F32
        )
        total = total + bias2[:, 256 * p : 256 * p + 256]
        for g in range(4):
            cut = pl.ds(GROUP * g + 256 * p, 256)
            out_ref[:, :, cut] = (
                x_ref[:, :, cut].astype(F32) + total[64 * g : 64 * g + 64].reshape(4, 16, 256)
            ).astype(BF)


SCRATCH = [
    pltpu.VMEM((640, GROUP), BF),
    pltpu.VMEM((640, GROUP), F32),
    pltpu.VMEM((3, 8, 16, WIDE), BF),
    pltpu.VMEM((6, 16, LANES), F32),
    pltpu.VMEM((3, 3, 16, WIDE), BF),
    pltpu.VMEM((448, GROUP), BF),
    pltpu.VMEM((3, 6, 16, WIDE), BF),
]


def vmem():
    return pl.BlockSpec(memory_space=pltpu.VMEM)


def make_pairs(tms, rws):
    def flat(move):
        pairs = []
        for t in range(tms):
            for r in range(rws):
                to_t, to_r = move(t, r)
                pairs.append((t * rws + r, to_t * rws + to_r))
        return pairs

    def odd(t, r):
        if r in (0, rws - 1):
            return t ^ 1, r
        return t, (r + 1 if r % 2 else r - 1)

    def later(t, r):
        return (t + 1) % tms, r

    def even(t, r):
        return t, r ^ 1

    return (
        flat(later),
        flat(even),
        flat(odd),
        flat(lambda t, r: later(*even(t, r))),
        flat(lambda t, r: ((t + 1) % tms, r) if r in (0, rws - 1) else later(*odd(t, r))),
    )


def block(frames, received, banded):
    near = [pltpu.with_memory_space_constraint(q, pltpu.VMEM) for q in (frames,) + tuple(received) + tuple(banded)]
    return pl.pallas_call(
        main_kernel,
        out_shape=jax.ShapeDtypeStruct((4, 16, LANES), BF),
        in_specs=[vmem()] * 13,
        out_specs=vmem(),
        scratch_shapes=SCRATCH,
        compiler_params=pltpu.CompilerParams(vmem_limit_bytes=24 << 20),
        name="block",
    )(*near)


def solution(mesh):
    later, even_swap, odd_swap, even_later, odd_later = make_pairs(mesh.shape["tm"], mesh.shape["rows"])
    axes = ("tm", "rows")

    def body(frames, gain_one, weight_one, bias_one, gain_two, weight_two, bias_two):
        prev = lax.ppermute(frames, axes, later)
        edge = pltpu.VMEM((8, LANES), BF)
        e0, e1 = pl.pallas_call(
            edges_kernel, out_shape=(edge, edge), in_specs=[vmem()], out_specs=(vmem(), vmem()), name="edges"
        )(frames)
        h0 = lax.ppermute(e0, axes, even_swap)
        h1 = lax.ppermute(e1, axes, odd_swap)
        c0 = lax.ppermute(e0, axes, even_later)
        c1 = lax.ppermute(e1, axes, odd_later)
        banded = bands(weight_one, weight_two, (gain_one, bias_one, gain_two, bias_two))
        return block(frames, (prev, h0, h1, c0, c1), banded)

    in_specs = (P("tm", "rows", None), P(), P(), P(), P(), P(), P())
    out_specs = P("tm", "rows", None)
    return jax.shard_map(body, mesh=mesh, in_specs=in_specs, out_specs=out_specs, check_vma=False)
```

time: 47.8 us -> 25.2 us (0.53)
  the two profiles are of different devices: /device:TPU:103 before, /device:TPU:133 now
where the time goes in v2:
time: 25.2 us; the launch traced here: 25 us
  Pallas kernels  15.3 us (61%)
  starting transfers between devices  9.7 us (38%)
    pallas_call x1, Pallas kernels, block(): pl.pallas_call(main_kernel, out_shape=jax.ShapeDtypeStruct((4, 16, LANES)...  9.83 us
    pallas_call x1, Pallas kernels, bands(): pl.pallas_call(band_kernel, out_shape=tuple((pltpu.VMEM((9, d, 256), BF)...  4.28 us
    ppermute x1, starting transfers between devices, body(): h1 = lax.ppermute(e1, axes, odd_swap)  3.63 us
    ppermute x1, starting transfers between devices, body(): c1 = lax.ppermute(e1, axes, odd_later)  3.12 us
    ppermute x1, starting transfers between devices, body(): prev = lax.ppermute(frames, axes, later)  1.48 us
    pallas_call x1, Pallas kernels, body(): pl.pallas_call(edges_kernel, out_shape=(edge, edge), in_specs=[vmem()], o...  1.16 us
    ppermute x1, starting transfers between devices, body(): c0 = lax.ppermute(e0, axes, even_later)  1.06 us
  transfers between devices with their start and end apart: 5, of which 0 were waited for; matrix products, arithmetic and copies ran while one was open for 0% of the time, Pallas kernels for 22%

profile of v2, /device:TPU:133, one launch (start us, length us, event | category | flops | bytes accessed | tf_op | source)
XLA Modules:
  0.0 25.0 jit_solution(12475735494507999650)
XLA Ops:
  0.0 1.5 %collective-permute-start = (bf16[4,16,3072]{2,1,0:T(8,128)(2,1)}, bf16[4,16,3072]{2,1,0:T(8,128)(2,1)S(1)}, u32[]{:S(2)}, u32[]{:S(2)}) collective-permute-start(bf16[4,16,3072]{2,1,0:T(8,128)(2,1)} %x_ref.3), channel_id=1, source_target_pairs={{0,16},{1,17},{2,18},{3,19},{4,20},{5,21},{6,22},{7,23},{8,24},{9,... | collective-permute-start | bytes 1179656 | tf_op jit(solution)/shard_map/ppermute | solution.py:324
  1.5 1.2 %edges.1 = (bf16[8,3072]{1,0:T(8,128)(2,1)S(1)}, bf16[8,3072]{1,0:T(8,128)(2,1)S(1)}) custom-call(bf16[4,16,3072]{2,1,0:T(8,128)(2,1)} %x_ref.3), custom_call_target="tpu_custom_call" | custom-call | tf_op jit(solution)/shard_map/edges/pallas_call | solution.py:326
  2.6 1.1 %collective-permute-start.3 = (bf16[8,3072]{1,0:T(8,128)(2,1)S(1)}, bf16[8,3072]{1,0:T(8,128)(2,1)S(1)}, u32[]{:S(2)}, u32[]{:S(2)}) collective-permute-start(bf16[8,3072]{1,0:T(8,128)(2,1)S(1)} %get-tuple-element.14), channel_id=1, source_target_pairs={{0,17},{1,16},{2,19},{3,18},{4,21},{5,20},{6,23},{7,22},{8,25},{9,... | collective-permute-start | bytes 147464 | tf_op jit(solution)/shard_map/ppermute | solution.py:331
  3.7 0.4 %collective-permute-start.1 = (bf16[8,3072]{1,0:T(8,128)(2,1)S(1)}, bf16[8,3072]{1,0:T(8,128)(2,1)S(1)}, u32[]{:S(2)}, u32[]{:S(2)}) collective-permute-start(bf16[8,3072]{1,0:T(8,128)(2,1)S(1)} %get-tuple-element.14), channel_id=1, source_target_pairs={{0,1},{1,0},{2,3},{3,2},{4,5},{5,4},{6,7},{7,6},{8,9},{9,8},{10,11... | collective-permute-start | bytes 147464 | tf_op jit(solution)/shard_map/ppermute | solution.py:329
  4.1 3.1 %collective-permute-start.4 = (bf16[8,3072]{1,0:T(8,128)(2,1)S(1)}, bf16[8,3072]{1,0:T(8,128)(2,1)S(1)}, u32[]{:S(2)}, u32[]{:S(2)}) collective-permute-start(bf16[8,3072]{1,0:T(8,128)(2,1)S(1)} %get-tuple-element.15), channel_id=1, source_target_pairs={{0,16},{1,18},{2,17},{3,20},{4,19},{5,22},{6,21},{7,24},{8,23},{9,... | collective-permute-start | bytes 147464 | tf_op jit(solution)/shard_map/ppermute | solution.py:332
  7.2 3.6 %collective-permute-start.2 = (bf16[8,3072]{1,0:T(8,128)(2,1)S(1)}, bf16[8,3072]{1,0:T(8,128)(2,1)S(1)}, u32[]{:S(2)}, u32[]{:S(2)}) collective-permute-start(bf16[8,3072]{1,0:T(8,128)(2,1)S(1)} %get-tuple-element.15), channel_id=1, source_target_pairs={{0,16},{1,2},{2,1},{3,4},{4,3},{5,6},{6,5},{7,8},{8,7},{9,10},{10,... | collective-permute-start | bytes 147464 | tf_op jit(solution)/shard_map/ppermute | solution.py:330
  10.9 0.0 copy-start
  10.9 4.3 %bands.1 = (bf16[9,512,256]{2,1,0:T(8,128)(2,1)S(1)}, bf16[9,768,256]{2,1,0:T(8,128)(2,1)S(1)}, bf16[9,512,256]{2,1,0:T(8,128)(2,1)S(1)}, bf16[9,512,256]{2,1,0:...) custom-call(bf16[3,9,96,96]{3,2,1,0:T(8,128)(2,1)} %bitcast.6, ...), custom_call_target="tpu_custom_call" | custom-call | flops 4000000000 | bytes 18000000 | tf_op jit(solution)/shard_map/bands/pallas_call | solution.py:96
  15.2 0.0 collective-permute-done.3.c0_ref
  15.2 0.0 collective-permute-done.1.h0_ref
  15.2 0.0 collective-permute-done.4.c1_ref
  15.2 0.0 collective-permute-done.2.h1_ref
  15.2 0.0 collective-permute-done.prev_ref
  15.2 0.0 copy-done
  15.2 9.8 %block.1 = bf16[4,16,3072]{2,1,0:T(8,128)(2,1)} custom-call(bf16[4,16,3072]{2,1,0:T(8,128)(2,1)S(1)} %copy-done, bf16[4,16,3072]{2,1,0:T(8,128)(2,1)S(1)} %collective-permute-done.prev_ref, bf16[8,3072]{1,0:T(8,128)(2,1)S(1)} %collective-permute-done.1.h0_ref, bf16[8,3072]{1,0:T(8,128)(2,1)S(1)} %collective-permute-done.2.h1_ref, ...), custom_call_target="tpu_custom_call" | custom-call | tf_op jit(solution)/shard_map/block/pallas_call | solution.py:308
Async XLA Ops:
  0.0 15.2 %collective-permute-start = (bf16[4,16,3072]{2,1,0:T(8,128)(2,1)}, bf16[4,16,3072]{2,1,0:T(8,128)(2,1)S(1)}, u32[]{:S(2)}, u32[]{:S(2)}) collective-permute-start(bf16[4,16,3072]{2,1,0:T(8,128)(2,1)} %x_ref.3), channel_id=1, source_target_pairs={{0,16},{1,17},{2,18},{3,19},{4,20},{5,21},{6,22},{7,23},{8,24},{9,... | collective-permute-start | bytes 1179656 | tf_op jit(solution)/shard_map/ppermute | solution.py:324
  2.6 12.5 %collective-permute-start.3 = (bf16[8,3072]{1,0:T(8,128)(2,1)S(1)}, bf16[8,3072]{1,0:T(8,128)(2,1)S(1)}, u32[]{:S(2)}, u32[]{:S(2)}) collective-permute-start(bf16[8,3072]{1,0:T(8,128)(2,1)S(1)} %get-tuple-element.14), channel_id=1, source_target_pairs={{0,17},{1,16},{2,19},{3,18},{4,21},{5,20},{6,23},{7,22},{8,25},{9,... | collective-permute-start | bytes 147464 | tf_op jit(solution)/shard_map/ppermute | solution.py:331
  3.7 11.5 %collective-permute-start.1 = (bf16[8,3072]{1,0:T(8,128)(2,1)S(1)}, bf16[8,3072]{1,0:T(8,128)(2,1)S(1)}, u32[]{:S(2)}, u32[]{:S(2)}) collective-permute-start(bf16[8,3072]{1,0:T(8,128)(2,1)S(1)} %get-tuple-element.14), channel_id=1, source_target_pairs={{0,1},{1,0},{2,3},{3,2},{4,5},{5,4},{6,7},{7,6},{8,9},{9,8},{10,11... | collective-permute-start | bytes 147464 | tf_op jit(solution)/shard_map/ppermute | solution.py:329
  4.1 11.1 %collective-permute-start.4 = (bf16[8,3072]{1,0:T(8,128)(2,1)S(1)}, bf16[8,3072]{1,0:T(8,128)(2,1)S(1)}, u32[]{:S(2)}, u32[]{:S(2)}) collective-permute-start(bf16[8,3072]{1,0:T(8,128)(2,1)S(1)} %get-tuple-element.15), channel_id=1, source_target_pairs={{0,16},{1,18},{2,17},{3,20},{4,19},{5,22},{6,21},{7,24},{8,23},{9,... | collective-permute-start | bytes 147464 | tf_op jit(solution)/shard_map/ppermute | solution.py:332
  7.2 8.0 %collective-permute-start.2 = (bf16[8,3072]{1,0:T(8,128)(2,1)S(1)}, bf16[8,3072]{1,0:T(8,128)(2,1)S(1)}, u32[]{:S(2)}, u32[]{:S(2)}) collective-permute-start(bf16[8,3072]{1,0:T(8,128)(2,1)S(1)} %get-tuple-element.15), channel_id=1, source_target_pairs={{0,16},{1,2},{2,1},{3,4},{4,3},{5,6},{6,5},{7,8},{8,7},{9,10},{10,... | collective-permute-start | bytes 147464 | tf_op jit(solution)/shard_map/ppermute | solution.py:330
  10.9 4.3 %copy-start = (bf16[4,16,3072]{2,1,0:T(8,128)(2,1)S(1)}, bf16[4,16,3072]{2,1,0:T(8,128)(2,1)}, u32[]{:S(2)}) copy-start(bf16[4,16,3072]{2,1,0:T(8,128)(2,1)} %x_ref.3) | copy-start | bytes 1179652

commit v3 on v2

v3 whole, which is shorter than its diff:
```python
import jax
import jax.numpy as jnp
from jax import lax
from jax.experimental import pallas as pl
from jax.experimental.pallas import tpu as pltpu
from jax.sharding import PartitionSpec as P

C = 96
GROUP = 768
PAD = 128
LANES = 3072
WIDE = LANES + 2 * PAD
STARTS = (-128, 0, 384)
DEPTHS = (512, 768, 512)
HALVES = (
    ((96, (32, 0), (128, 96)), (64, (128, 96), (224, 64))),
    ((32, (96, 64), (192, 32)), (96, (288, 0), (384, 96))),
    ((64, (0, 96), (96, 64)), (32, (96, 64), (192, 32))),
)
BF = jnp.bfloat16
F32 = jnp.float32


def fetch_kernel(x_hbm, e0_ref, e1_ref, x_ref, sems):
    copies = [pltpu.make_async_copy(x_hbm.at[f], x_ref.at[f], sems.at[f]) for f in range(4)]
    for copy in copies:
        copy.start()
    even = lax.rem(lax.axis_index("rows"), 2) == 0
    spot = lax.broadcasted_iota(jnp.int32, (8, LANES), 0)
    top, bot = jnp.zeros((8, LANES), F32), jnp.zeros((8, LANES), F32)
    for f in range(4):
        copies[f].wait()
        head = x_ref[f, 0:8, :].astype(F32)
        tail = x_ref[f, 8:16, :].astype(F32)
        for row in range(2):
            here = spot == 4 * row + f
            top = jnp.where(here, head[row : row + 1], top)
            bot = jnp.where(here, tail[6 + row : 7 + row], bot)
    e0_ref[...] = jnp.where(even, bot, top).astype(BF)
    e1_ref[...] = jnp.where(even, top, bot).astype(BF)


def fetch(frames):
    edge = pltpu.VMEM((8, LANES), BF)
    return pl.pallas_call(
        fetch_kernel,
        out_shape=(edge, edge, pltpu.VMEM((4, 16, LANES), BF)),
        in_specs=[pl.BlockSpec(memory_space=pltpu.HBM)],
        out_specs=(vmem(),) * 3,
        scratch_shapes=[pltpu.SemaphoreType.DMA((4,))],
        compiler_params=pltpu.CompilerParams(vmem_limit_bytes=4 << 20),
        name="fetch",
    )(pltpu.with_memory_space_constraint(frames, pltpu.HBM))


def band_fill(out, p):
    for half in range(2):
        first = HALVES[p][half][1][0]
        cut = slice(128 * half, 128 * half + 128)
        if first:
            out[:, 0:first, cut] = jnp.zeros((9, first, 128), BF)
        end = first + 4 * C
        if end < DEPTHS[p]:
            out[:, end : DEPTHS[p], cut] = jnp.zeros((9, DEPTHS[p] - end, 128), BF)


def band_taps(w_ref, outs, taps):
    lane = lax.broadcasted_iota(jnp.int32, (C, 128), 1)
    none = jnp.zeros((C, 128), BF)
    for k in taps:
        blocks = []
        for kw in range(3):
            wide = jnp.concatenate([w_ref[3 * k + kw].astype(F32), jnp.zeros((C, 32), F32)], axis=1)
            blocks.append({r: (pltpu.roll(wide, r, 1) if r else wide).astype(BF) for r in (0, 32, 64, 96)})
        for p, out in outs:
            for half in range(2):
                edge, left, right = HALVES[p][half]
                for d in range(4):
                    a = blocks[d][left[1]] if d < 3 else none
                    b = blocks[d - 1][right[1]] if d else none
                    row = left[0] + C * d
                    out[k, row : row + C, 128 * half : 128 * half + 128] = jnp.where(lane < edge, a, b)


def band_kernel(
    w1_ref, w2_ref, p0, p1, p2, p3, o0, o1, o2, q0, q1, q2, par_ref, buf, small, sems, small_sems
):
    copies = []
    for n, ref in enumerate((w1_ref, w2_ref)):
        copies.append(pltpu.make_async_copy(ref, buf.at[n], sems.at[n]))
    tiny = [pltpu.make_async_copy(ref, small.at[n], small_sems.at[n]) for n, ref in enumerate((p0, p1, p2, p3))]
    for copy in copies + tiny:
        copy.start()
    both = [list(enumerate(refs)) for refs in ((o0, o1, o2), (q0, q1, q2))]
    for outs in both:
        for p, out in outs:
            band_fill(out, p)
    for n, outs in enumerate(both):
        copies[n].wait()
        band_taps(buf.at[n], outs, range(9))
    for copy in tiny:
        copy.wait()
    params = [0.5 * small[0], small[1], 0.5 * small[2], small[3]]
    par_ref[...] = jnp.concatenate([jnp.concatenate(params, axis=0)] * (GROUP // C), axis=1)


def bands(weight_one, weight_two, params):
    far = [w.reshape(27, C, C) for w in (weight_one, weight_two)] + [q.reshape(1, C) for q in params]
    return pl.pallas_call(
        band_kernel,
        out_shape=tuple(pltpu.VMEM((9, d, 256), BF) for d in DEPTHS * 2) + (pltpu.VMEM((4, GROUP), F32),),
        in_specs=[pl.BlockSpec(memory_space=pltpu.HBM)] * 6,
        out_specs=(vmem(),) * 7,
        scratch_shapes=[
            pltpu.VMEM((2, 27, C, C), BF),
            pltpu.VMEM((4, 1, C), F32),
            pltpu.SemaphoreType.DMA((2,)),
            pltpu.SemaphoreType.DMA((4,)),
        ],
        compiler_params=pltpu.CompilerParams(vmem_limit_bytes=8 << 20),
        cost_estimate=pl.CostEstimate(flops=4000000000, bytes_accessed=18000000, transcendentals=0),
        name="bands",
    )(*[pltpu.with_memory_space_constraint(q, pltpu.HBM) for q in far])


def one_hots():
    lane = lax.broadcasted_iota(jnp.int32, (GROUP, 256), 0)
    col = lax.broadcasted_iota(jnp.int32, (GROUP, 256), 1) * C
    gather = jnp.where((lane >= col) & (lane < col + C), 1.0, 0.0).astype(BF)
    lane = lax.broadcasted_iota(jnp.int32, (256, GROUP), 1)
    col = lax.rem(lax.broadcasted_iota(jnp.int32, (256, GROUP), 0), 128) * C
    spread = jnp.where((lane >= col) & (lane < col + C), 1.0, 0.0).astype(BF)
    return gather, spread


def norm(square, scale, count, gather, spread):
    half = count // 2

    def run(*accs):
        for k in range(3):
            for unit in range(2):
                pltpu.matmul_push_rhs(gather[256 * k : 256 * k + 256, :], k % 2, unit)
                lhs = square[half * unit : half * unit + half, 256 * k : 256 * k + 256]
                pltpu.matmul_acc_lhs(accs[unit], lhs, load_staged_rhs=k % 2)
        for unit in range(2):
            total = pltpu.matmul_pop(accs[unit])[:, 0:128]
            r = lax.rsqrt(total * (1.0 / C) + 1e-06)
            high = r.astype(BF)
            low = (r - high.astype(F32)).astype(BF)
            lhs = jnp.concatenate([high, low], axis=1)
            for n in range(3):
                stage = (n + 1) % 2
                pltpu.matmul_push_rhs(spread[:, 256 * n : 256 * n + 256], stage, unit)
                pltpu.matmul_acc_lhs(accs[unit], lhs, load_staged_rhs=stage)
                scale[half * unit : half * unit + half, 256 * n : 256 * n + 256] = pltpu.matmul_pop(accs[unit])

    pl.run_scoped(run, *[pltpu.ACC(n)((half, 256), F32) for n in range(2)])


def act(v, scale, gain):
    half = v.astype(F32) * scale * gain
    return half + half * jnp.tanh(half)


def zero_sides(ref):
    shape = ref.shape[:-1]
    ref[..., pl.ds(0, PAD)] = jnp.zeros(shape + (PAD,), BF)
    ref[..., pl.ds(PAD + LANES, PAD)] = jnp.zeros(shape + (PAD,), BF)


def shifted(ref, f, g, v, above, below):
    cut = pl.ds(PAD + GROUP * g, GROUP)
    ref[0, f, :, cut] = jnp.concatenate([above, v[0:15]], axis=0).astype(BF)
    ref[1, f, :, cut] = v.astype(BF)
    ref[2, f, :, cut] = jnp.concatenate([v[1:16], below], axis=0).astype(BF)


def groups(ref, index, p, sub):
    lanes = [pl.ds(PAD + GROUP * g + STARTS[p] + 256 * sub, 256) for g in range(4)]
    return jnp.concatenate([ref[index + (slice(None), cut)] for cut in lanes], axis=0)


def convolve(p, weight, users, count):
    def run(*accs):
        step = 0
        for kt in range(3):
            for kh in range(3):
                for sub in range(DEPTHS[p] // 256):
                    unit, stage = step % 2, (step // 2) % 2
                    step += 1
                    pltpu.matmul_push_rhs(weight[3 * kt + kh, 256 * sub : 256 * sub + 256, :], stage, unit)
                    load = stage
                    for chunk, ref, index in users(kt, kh):
                        pltpu.matmul_acc_lhs(
                            accs[2 * chunk + unit], groups(ref, index, p, sub), load_staged_rhs=load
                        )
                        load = None
        return [pltpu.matmul_pop(accs[2 * c]) + pltpu.matmul_pop(accs[2 * c + 1]) for c in range(count)]

    return pl.run_scoped(run, *[pltpu.ACC(n % 2)((64, 256), F32) for n in range(2 * count)])


def inner_kernel(
    x_ref, prev_ref, u0, u1, u2, par_ref, packed_ref, part_ref, ends_ref, gather, spread, a1, square, scale
):
    del packed_ref
    older = lax.axis_index("tm") > 0
    gather[...], spread[...] = one_hots()
    gain1 = par_ref[0:1, :]
    zero_sides(a1)
    zero = jnp.zeros((), BF)
    for g in range(4):
        cut = pl.ds(GROUP * g, GROUP)
        before = jnp.where(older, prev_ref[:, :, cut].reshape(64, GROUP), zero)
        own = x_ref[:, :, cut].reshape(64, GROUP)
        square[128 * g : 128 * g + 64, :] = before * before
        square[128 * g + 64 : 128 * g + 128, :] = own * own
    norm(square, scale, 512, gather, spread)
    none = jnp.zeros((1, GROUP), F32)
    for g in range(4):
        cut = pl.ds(GROUP * g, GROUP)
        for f in range(8):
            if f < 4:
                v = jnp.where(older, prev_ref[f, :, cut], zero)
            else:
                v = x_ref[f - 4, :, cut]
            v = act(v, scale[pl.ds(128 * g + 16 * f, 16), :], gain1)
            shifted(a1, f, g, v, none, none)
            ends_ref[0, f : f + 1, cut] = v[0:1]
            ends_ref[1, f : f + 1, cut] = v[15:16]
    for p, w in enumerate((u0, u1, u2)):
        totals = convolve(p, w, lambda kt, kh: [(f, a1, (kh, f + kt)) for f in range(6)], 6)
        for f, total in enumerate(totals):
            part_ref[64 * f : 64 * f + 64, pl.ds(256 * p, 256)] = total


def main_kernel(
    x_ref, h0_ref, h1_ref, c_ref,
    part_ref, ends_ref, gather, spread, u0, u1, u2, v0, v1, v2, par_ref, out_ref,
    square, scale, e, et, hid, a2,
):
    tm = lax.axis_index("tm")
    rows = lax.axis_index("rows")
    even = lax.rem(rows, 2) == 0
    older = tm > 0
    zero_sides(et)
    zero_sides(a2)
    gain1 = par_ref[0:1, :]
    bias1 = par_ref[1:2, :]
    gain2 = par_ref[2:3, :]
    bias2 = par_ref[3:4, :]

    for g in range(4):
        cut = pl.ds(GROUP * g, GROUP)
        h0, h1 = h0_ref[:, cut].astype(F32), h1_ref[:, cut].astype(F32)
        c0, c1 = c_ref[0:8, cut].astype(F32), c_ref[8:16, cut].astype(F32)
        up = jnp.where(rows > 0, jnp.where(even, h1, h0), 0.0)
        down = jnp.where(rows < 15, jnp.where(even, h0, h1), 0.0)
        up_old = jnp.where((rows > 0) & older, jnp.where(even, c1, c0), 0.0)
        down_old = jnp.where((rows < 15) & older, jnp.where(even, c0, c1), 0.0)
        halo = jnp.concatenate([up_old, up, down_old, down], axis=0).astype(BF)
        e[0, 0:8, cut] = up_old
        e[1, 0:8, cut] = up
        e[4, 0:8, cut] = down_old
        e[5, 0:8, cut] = down
        square[32 * g : 32 * g + 32, :] = halo * halo
    norm(square, scale, 128, gather, spread)
    for g in range(4):
        cut = pl.ds(GROUP * g, GROUP)

        def halo_act(q, n):
            return act(e[q, 0:8, cut], scale[pl.ds(32 * g + 8 * n, 8), :], gain1)

        up_old, up, down_old, down = halo_act(0, 0), halo_act(1, 1), halo_act(4, 2), halo_act(5, 3)
        e[0, 0:8, cut] = jnp.concatenate([up_old[0:4], up[0:4]], axis=0)
        e[1, 0:8, cut] = jnp.concatenate([up_old[4:8], up[4:8]], axis=0)
        e[4, 0:8, cut] = jnp.concatenate([down_old[0:4], down[0:4]], axis=0)
        e[5, 0:8, cut] = jnp.concatenate([down_old[4:8], down[4:8]], axis=0)
        e[2, 0:8, cut] = ends_ref[0, :, cut]
        e[3, 0:8, cut] = ends_ref[1, :, cut]
        for kt in range(3):
            for kh in range(3):
                et[kt, kh, :, pl.ds(PAD + GROUP * g, GROUP)] = jnp.concatenate(
                    [e[kh, kt : kt + 8, cut], e[3 + kh, kt : kt + 8, cut]], axis=0
                ).astype(BF)

    spot = lax.broadcasted_iota(jnp.int32, (16, 256), 0)
    for p, w in enumerate((u0, u1, u2)):

        def users(kt, kh):
            chunks = [(0, et, (kt, kh))]
            if kh != 1:
                chunks.append((1 + kh // 2, et, (kt, 1)))
            return chunks

        lanes = pl.ds(256 * p, 256)
        outside, first, last = convolve(p, w, users, 3)
        bias = bias1[:, 256 * p : 256 * p + 256]
        for f in range(6):
            for g in range(4):
                add = jnp.where(
                    spot == 0,
                    first[16 * g + f : 16 * g + f + 1],
                    jnp.where(spot == 15, last[16 * g + 8 + f : 16 * g + 9 + f], 0.0),
                )
                at = pl.ds(64 * f + 16 * g, 16)
                total = (part_ref[at, lanes] + add + bias).astype(BF)
                hid[at, lanes] = total
                square[at, lanes] = total * total
        total = (outside + bias).astype(BF)
        hid[384:448, lanes] = total
        square[384:448, lanes] = total * total

    norm(square, scale, 448, gather, spread)
    spot = lax.broadcasted_iota(jnp.int32, (16, GROUP), 0)
    frame = lax.rem(spot, 8)
    keep = ((spot >= 8) | (rows > 0)) & ((spot < 8) | (rows < 15)) & ((frame >= 2) | older)
    for g in range(4):
        cut = pl.ds(GROUP * g, GROUP)
        at = pl.ds(384 + 16 * g, 16)
        e[0, :, cut] = jnp.where(keep, act(hid[at, :], scale[at, :], gain2), 0.0)
        for f in range(6):
            at = pl.ds(64 * f + 16 * g, 16)
            v = act(hid[at, :], scale[at, :], gain2)
            if f < 2:
                v = jnp.where(older, v, 0.0)
            shifted(a2, f, g, v, e[0, f : f + 1, cut], e[0, 8 + f : 9 + f, cut])

    for p, w in enumerate((v0, v1, v2)):
        totals = convolve(p, w, lambda kt, kh: [(f, a2, (kh, f + kt)) for f in range(4)], 4)
        for f, total in enumerate(totals):
            total = total + bias2[:, 256 * p : 256 * p + 256]
            for g in range(4):
                cut = pl.ds(GROUP * g + 256 * p, 256)
                out_ref[f, :, cut] = (x_ref[f, :, cut].astype(F32) + total[16 * g : 16 * g + 16]).astype(BF)


SCRATCH = [
    pltpu.VMEM((448, GROUP), BF),
    pltpu.VMEM((448, GROUP), F32),
    pltpu.VMEM((6, 16, LANES), F32),
    pltpu.VMEM((3, 3, 16, WIDE), BF),
    pltpu.VMEM((448, GROUP), BF),
    pltpu.VMEM((3, 6, 16, WIDE), BF),
]


def pack_kernel(h0_ref, h1_ref, par_ref, packed_ref):
    del par_ref
    packed_ref[0:8, :] = h0_ref[...]
    packed_ref[8:16, :] = h1_ref[...]


def pack(*arrays):
    return pl.pallas_call(
        pack_kernel,
        out_shape=pltpu.VMEM((16, LANES), BF),
        in_specs=[vmem()] * 3,
        out_specs=vmem(),
        compiler_params=pltpu.CompilerParams(vmem_limit_bytes=1 << 20),
        name="pack",
    )(*[pltpu.with_memory_space_constraint(q, pltpu.VMEM) for q in arrays])


def inner(*arrays):
    return pl.pallas_call(
        inner_kernel,
        out_shape=(
            pltpu.VMEM((384, GROUP), F32),
            pltpu.VMEM((2, 8, LANES), F32),
            pltpu.VMEM((GROUP, 256), BF),
            pltpu.VMEM((256, GROUP), BF),
        ),
        in_specs=[vmem()] * 7,
        out_specs=(vmem(),) * 4,
        scratch_shapes=[
            pltpu.VMEM((3, 8, 16, WIDE), BF),
            pltpu.VMEM((512, GROUP), BF),
            pltpu.VMEM((512, GROUP), F32),
        ],
        compiler_params=pltpu.CompilerParams(vmem_limit_bytes=12 << 20),
        cost_estimate=pl.CostEstimate(flops=4000000000, bytes_accessed=18000000, transcendentals=0),
        name="inner",
    )(*[pltpu.with_memory_space_constraint(q, pltpu.VMEM) for q in arrays])


def vmem():
    return pl.BlockSpec(memory_space=pltpu.VMEM)


def make_pairs(tms, rws):
    def flat(move):
        pairs = []
        for t in range(tms):
            for r in range(rws):
                to_t, to_r = move(t, r)
                pairs.append((t * rws + r, to_t * rws + to_r))
        return pairs

    def even(t, r):
        return t, r ^ 1

    def odd(t, r):
        if r in (0, rws - 1):
            return t ^ 1, r
        return t, (r + 1 if r % 2 else r - 1)

    def later(t, r):
        return (t + 1, r) if t < tms - 1 else (0, r ^ 1)

    return tuple(flat(move) for move in (later, even, odd))


def block(*arrays):
    near = [pltpu.with_memory_space_constraint(q, pltpu.VMEM) for q in arrays]
    return pl.pallas_call(
        main_kernel,
        out_shape=jax.ShapeDtypeStruct((4, 16, LANES), BF),
        in_specs=[vmem()] * 15,
        out_specs=vmem(),
        scratch_shapes=SCRATCH,
        compiler_params=pltpu.CompilerParams(vmem_limit_bytes=16 << 20),
        name="block",
    )(*near)


def solution(mesh):
    later, even_swap, odd_swap = make_pairs(mesh.shape["tm"], mesh.shape["rows"])
    axes = ("tm", "rows")

    def body(frames, gain_one, weight_one, bias_one, gain_two, weight_two, bias_two):
        prev = lax.ppermute(frames, axes, later)
        e0, e1, near = fetch(frames)
        h0 = lax.ppermute(e0, axes, even_swap)
        h1 = lax.ppermute(e1, axes, odd_swap)
        banded = bands(weight_one, weight_two, (gain_one, bias_one, gain_two, bias_two))
        packed = pack(h0, h1, banded[6])
        corners = lax.ppermute(packed, axes, later)
        partial = inner(near, prev, *banded[:3], banded[6], packed)
        return block(near, h0, h1, corners, *partial, *banded)

    in_specs = (P("tm", "rows", None), P(), P(), P(), P(), P(), P())
    out_specs = P("tm", "rows", None)
    return jax.shard_map(body, mesh=mesh, in_specs=in_specs, out_specs=out_specs, check_vma=False)
```

time: 25.2 us -> 23.7 us (0.940)
  the two profiles are of different devices: /device:TPU:133 before, /device:TPU:128 now
where the time goes in v3:
time: 23.7 us; the launch traced here: 23.6 us
  Pallas kernels  14.6 us (62%)
  waiting for transfers between devices  6.67 us (28%)
  starting transfers between devices  2.33 us (10%)
    pallas_call x1, Pallas kernels, block(): pl.pallas_call(main_kernel, out_shape=jax.ShapeDtypeStruct((4, 16, LANES)...  5.99 us
    pallas_call x1, Pallas kernels, inner(): pl.pallas_call(inner_kernel, out_shape=(pltpu.VMEM((384, GROUP), F32), pl...  4.64 us
    ppermute x1, waiting for transfers between devices, body(): h1 = lax.ppermute(e1, axes, odd_swap)  4.35 us
    pallas_call x1, Pallas kernels, bands(): pl.pallas_call(band_kernel, out_shape=tuple((pltpu.VMEM((9, d, 256), BF)...  2.82 us
    ppermute x1, waiting for transfers between devices, body(): corners = lax.ppermute(packed, axes, later)  2.24 us
    ppermute x1, starting transfers between devices, body(): h0 = lax.ppermute(e0, axes, even_swap)  1.66 us
    pallas_call x1, Pallas kernels, fetch(): pl.pallas_call(fetch_kernel, out_shape=(edge, edge, pltpu.VMEM((4, 16, LA...  1.11 us
    ppermute x1, starting transfers between devices, body(): corners = lax.ppermute(packed, axes, later)  0.66 us
  transfers between devices with their start and end apart: 4, of which 3 were waited for; matrix products, arithmetic and copies ran while one was open for 0% of the time, Pallas kernels for 36%

profile of v3, /device:TPU:128, one launch (start us, length us, event | category | flops | bytes accessed | tf_op | source)
XLA Modules:
  0.0 23.6 jit_solution(11567891931297823155)
XLA Ops:
  0.0 0.0 collective-permute-start.3
  0.0 1.1 %fetch.1 = (bf16[8,3072]{1,0:T(8,128)(2,1)S(1)}, bf16[8,3072]{1,0:T(8,128)(2,1)S(1)}, bf16[4,16,3072]{2,1,0:T(8,128)(2,1)S(1)}) custom-call(bf16[4,16,3072]{2,1,0:T(8,128)(2,1)} %x_hbm.1), custom_call_target="tpu_custom_call" | custom-call | tf_op jit(solution)/shard_map/fetch/pallas_call | solution.py:45
  1.1 1.7 %collective-permute-start = (bf16[8,3072]{1,0:T(8,128)(2,1)S(1)}, bf16[8,3072]{1,0:T(8,128)(2,1)S(1)}, u32[]{:S(2)}, u32[]{:S(2)}) collective-permute-start(bf16[8,3072]{1,0:T(8,128)(2,1)S(1)} %get-tuple-element.20), channel_id=1, source_target_pairs={{0,1},{1,0},{2,3},{3,2},{4,5},{5,4},{6,7},{7,6},{8,9},{9,8},{10,11... | collective-permute-start | bytes 147464 | tf_op jit(solution)/shard_map/ppermute | solution.py:434
  2.8 0.0 collective-permute-start.1
  2.8 2.8 %bands.1 = (bf16[9,512,256]{2,1,0:T(8,128)(2,1)S(1)}, bf16[9,768,256]{2,1,0:T(8,128)(2,1)S(1)}, bf16[9,512,256]{2,1,0:T(8,128)(2,1)S(1)}, bf16[9,512,256]{2,1,0:...) custom-call(bf16[27,96,96]{2,1,0:T(8,128)(2,1)} %bitcast.6, ...), custom_call_target="tpu_custom_call" | custom-call | flops 4000000000 | bytes 18000000 | tf_op jit(solution)/shard_map/bands/pallas_call | solution.py:109
  5.6 0.0 collective-permute-done.h0_ref
  5.6 4.4 %collective-permute-done.1.h1_ref = bf16[8,3072]{1,0:T(8,128)(2,1)S(1)} collective-permute-done((bf16[8,3072]{1,0:T(8,128)(2,1)S(1)}, bf16[8,3072]{1,0:T(8,128)(2,1)S(1)}, u32[]{:S(2)}, u32[]{:S(2)}) %collective-permute-start.1) | collective-permute-done | bytes 49184 | tf_op jit(solution)/shard_map/ppermute | solution.py:435
  10.0 0.7 %collective-permute-start.2 = (bf16[16,3072]{1,0:T(8,128)(2,1)S(1)}, bf16[16,3072]{1,0:T(8,128)(2,1)S(1)}, u32[]{:S(2)}, u32[]{:S(2)}) collective-permute-start(bf16[16,3072]{1,0:T(8,128)(2,1)S(1)} %pack.1.packed_ref), channel_id=1, source_target_pairs={{0,16},{1,17},{2,18},{3,19},{4,20},{5,21},{6,22},{7,23},{8,24},{9,... | collective-permute-start | bytes 294920 | tf_op jit(solution)/shard_map/ppermute | solution.py:438
  10.7 0.1 collective-permute-done.3.prev_ref
  10.7 4.6 %inner.1 = (f32[384,768]{1,0:T(8,128)S(1)}, f32[2,8,3072]{2,1,0:T(8,128)S(1)}, bf16[768,256]{1,0:T(8,128)(2,1)S(1)}, bf16[256,768]{1,0:T(8,128)(2,1)S(1)}) custom-call(bf16[4,16,3072]{2,1,0:T(8,128)(2,1)S(1)} %get-tuple-element.19.x_ref, bf16[4,16,3072]{2,1,0:T(8,128)(2,1)S(1)} %collective-permute-done.3.prev_ref, ...), custom_call_target="tpu_custom_call" | custom-call | flops 4000000000 | bytes 18000000 | tf_op jit(solution)/shard_map/inner/pallas_call | solution.py:366
  15.4 2.2 %collective-permute-done.2.c_ref = bf16[16,3072]{1,0:T(8,128)(2,1)S(1)} collective-permute-done((bf16[16,3072]{1,0:T(8,128)(2,1)S(1)}, bf16[16,3072]{1,0:T(8,128)(2,1)S(1)}, u32[]{:S(2)}, u32[]{:S(2)}) %collective-permute-start.2) | collective-permute-done | bytes 98336 | tf_op jit(solution)/shard_map/ppermute | solution.py:438
  17.6 6.0 %block.1 = bf16[4,16,3072]{2,1,0:T(8,128)(2,1)} custom-call(bf16[4,16,3072]{2,1,0:T(8,128)(2,1)S(1)} %get-tuple-element.19.x_ref, bf16[8,3072]{1,0:T(8,128)(2,1)S(1)} %collective-permute-done.h0_ref, bf16[8,3072]{1,0:T(8,128)(2,1)S(1)} %collective-permute-done.1.h1_ref, bf16[16,3072]{1,0:T(8,128)(2,1)S(1)} %collective-permute-done.2.c_ref, ...), custom_call_target="tpu_custom_call" | custom-call | tf_op jit(solution)/shard_map/block/pallas_call | solution.py:416
  (1 shorter events, 0.0 us)
Async XLA Ops:
  0.0 10.7 %collective-permute-start.3 = (bf16[4,16,3072]{2,1,0:T(8,128)(2,1)}, bf16[4,16,3072]{2,1,0:T(8,128)(2,1)S(1)}, u32[]{:S(2)}, u32[]{:S(2)}) collective-permute-start(bf16[4,16,3072]{2,1,0:T(8,128)(2,1)} %x_hbm.1), channel_id=1, source_target_pairs={{0,16},{1,17},{2,18},{3,19},{4,20},{5,21},{6,22},{7,23},{8,24},{9,... | collective-permute-start | bytes 1179656 | tf_op jit(solution)/shard_map/ppermute | solution.py:432
  1.1 4.5 %collective-permute-start = (bf16[8,3072]{1,0:T(8,128)(2,1)S(1)}, bf16[8,3072]{1,0:T(8,128)(2,1)S(1)}, u32[]{:S(2)}, u32[]{:S(2)}) collective-permute-start(bf16[8,3072]{1,0:T(8,128)(2,1)S(1)} %get-tuple-element.20), channel_id=1, source_target_pairs={{0,1},{1,0},{2,3},{3,2},{4,5},{5,4},{6,7},{7,6},{8,9},{9,8},{10,11... | collective-permute-start | bytes 147464 | tf_op jit(solution)/shard_map/ppermute | solution.py:434
  2.8 7.2 %collective-permute-start.1 = (bf16[8,3072]{1,0:T(8,128)(2,1)S(1)}, bf16[8,3072]{1,0:T(8,128)(2,1)S(1)}, u32[]{:S(2)}, u32[]{:S(2)}) collective-permute-start(bf16[8,3072]{1,0:T(8,128)(2,1)S(1)} %get-tuple-element.21), channel_id=1, source_target_pairs={{0,16},{1,2},{2,1},{3,4},{4,3},{5,6},{6,5},{7,8},{8,7},{9,10},{10,... | collective-permute-start | bytes 147464 | tf_op jit(solution)/shard_map/ppermute | solution.py:435
  10.0 7.6 %collective-permute-start.2 = (bf16[16,3072]{1,0:T(8,128)(2,1)S(1)}, bf16[16,3072]{1,0:T(8,128)(2,1)S(1)}, u32[]{:S(2)}, u32[]{:S(2)}) collective-permute-start(bf16[16,3072]{1,0:T(8,128)(2,1)S(1)} %pack.1.packed_ref), channel_id=1, source_target_pairs={{0,16},{1,17},{2,18},{3,19},{4,20},{5,21},{6,22},{7,23},{8,24},{9,... | collective-permute-start | bytes 294920 | tf_op jit(solution)/shard_map/ppermute | solution.py:438

commit v4 on v3

--- a/solution.py
+++ b/solution.py
@@ -12,11 +12,8 @@
 WIDE = LANES + 2 * PAD
 STARTS = (-128, 0, 384)
 DEPTHS = (512, 768, 512)
-HALVES = (
-    ((96, (32, 0), (128, 96)), (64, (128, 96), (224, 64))),
-    ((32, (96, 64), (192, 32)), (96, (288, 0), (384, 96))),
-    ((64, (0, 96), (96, 64)), (32, (96, 64), (192, 32))),
-)
+STRIPS = ((96, 0, 96), (64, 96, 64), (32, 64, 32))
+STRIP_ROWS = ((32, 128), (96, 288), (0, 96))
 BF = jnp.bfloat16
 F32 = jnp.float32
 
@@ -53,18 +50,7 @@
     )(pltpu.with_memory_space_constraint(frames, pltpu.HBM))
 
 
-def band_fill(out, p):
-    for half in range(2):
-        first = HALVES[p][half][1][0]
-        cut = slice(128 * half, 128 * half + 128)
-        if first:
-            out[:, 0:first, cut] = jnp.zeros((9, first, 128), BF)
-        end = first + 4 * C
-        if end < DEPTHS[p]:
-            out[:, end : DEPTHS[p], cut] = jnp.zeros((9, DEPTHS[p] - end, 128), BF)
-
-
-def band_taps(w_ref, outs, taps):
+def strips(w_ref, out, taps):
     lane = lax.broadcasted_iota(jnp.int32, (C, 128), 1)
     none = jnp.zeros((C, 128), BF)
     for k in taps:
@@ -72,32 +58,42 @@
         for kw in range(3):
             wide = jnp.concatenate([w_ref[3 * k + kw].astype(F32), jnp.zeros((C, 32), F32)], axis=1)
             blocks.append({r: (pltpu.roll(wide, r, 1) if r else wide).astype(BF) for r in (0, 32, 64, 96)})
-        for p, out in outs:
-            for half in range(2):
-                edge, left, right = HALVES[p][half]
-                for d in range(4):
-                    a = blocks[d][left[1]] if d < 3 else none
-                    b = blocks[d - 1][right[1]] if d else none
-                    row = left[0] + C * d
-                    out[k, row : row + C, 128 * half : 128 * half + 128] = jnp.where(lane < edge, a, b)
-
-
-def band_kernel(
-    w1_ref, w2_ref, p0, p1, p2, p3, o0, o1, o2, q0, q1, q2, par_ref, buf, small, sems, small_sems
-):
+        for n, (edge, left, right) in enumerate(STRIPS):
+            for d in range(4):
+                a = blocks[d][left] if d < 3 else none
+                b = blocks[d - 1][right] if d else none
+                out[k, n, C * d : C * d + C, :] = jnp.where(lane < edge, a, b)
+
+
+def weight_tile(ref, k, p, sub):
+    halves = []
+    for half in range(2):
+        low = 256 * sub - STRIP_ROWS[p][half]
+        high = low + 256
+        parts = []
+        if low < 0:
+            parts.append(jnp.zeros((min(-low, 256), 128), BF))
+        if low < 4 * C and high > 0:
+            parts.append(ref[k, (2 * p + half) % 3, max(low, 0) : min(high, 4 * C), :])
+        if high > 4 * C:
+            parts.append(jnp.zeros((min(high - 4 * C, 256), 128), BF))
+        halves.append(jnp.concatenate(parts, axis=0))
+    return jnp.concatenate(halves, axis=1)
+
+
+def band_kernel(w1_ref, w2_ref, p0, p1, p2, p3, u_ref, v_ref, par_ref, buf, small, sems, small_sems):
     copies = []
     for n, ref in enumerate((w1_ref, w2_ref)):
-        copies.append(pltpu.make_async_copy(ref, buf.at[n], sems.at[n]))
+        for kt in range(3):
+            part = pl.ds(9 * kt, 9)
+            copies.append(pltpu.make_async_copy(ref.at[part], buf.at[n, part], sems.at[n, kt]))
     tiny = [pltpu.make_async_copy(ref, small.at[n], small_sems.at[n]) for n, ref in enumerate((p0, p1, p2, p3))]
     for copy in copies + tiny:
         copy.start()
-    both = [list(enumerate(refs)) for refs in ((o0, o1, o2), (q0, q1, q2))]
-    for outs in both:
-        for p, out in outs:
-            band_fill(out, p)
-    for n, outs in enumerate(both):
-        copies[n].wait()
-        band_taps(buf.at[n], outs, range(9))
+    for n, out in enumerate((u_ref, v_ref)):
+        for kt in range(3):
+            copies[3 * n + kt].wait()
+            strips(buf.at[n], out, range(3 * kt, 3 * kt + 3))
     for copy in tiny:
         copy.wait()
     params = [0.5 * small[0], small[1], 0.5 * small[2], small[3]]
@@ -106,15 +102,16 @@
 
 def bands(weight_one, weight_two, params):
     far = [w.reshape(27, C, C) for w in (weight_one, weight_two)] + [q.reshape(1, C) for q in params]
+    strip = pltpu.VMEM((9, 3, 4 * C, 128), BF)
     return pl.pallas_call(
         band_kernel,
-        out_shape=tuple(pltpu.VMEM((9, d, 256), BF) for d in DEPTHS * 2) + (pltpu.VMEM((4, GROUP), F32),),
+        out_shape=(strip, strip, pltpu.VMEM((4, GROUP), F32)),
         in_specs=[pl.BlockSpec(memory_space=pltpu.HBM)] * 6,
-        out_specs=(vmem(),) * 7,
+        out_specs=(vmem(),) * 3,
         scratch_shapes=[
             pltpu.VMEM((2, 27, C, C), BF),
             pltpu.VMEM((4, 1, C), F32),
-            pltpu.SemaphoreType.DMA((2,)),
+            pltpu.SemaphoreType.DMA((2, 3)),
             pltpu.SemaphoreType.DMA((4,)),
         ],
         compiler_params=pltpu.CompilerParams(vmem_limit_bytes=8 << 20),
@@ -188,7 +185,7 @@
                 for sub in range(DEPTHS[p] // 256):
                     unit, stage = step % 2, (step // 2) % 2
                     step += 1
-                    pltpu.matmul_push_rhs(weight[3 * kt + kh, 256 * sub : 256 * sub + 256, :], stage, unit)
+                    pltpu.matmul_push_rhs(weight_tile(weight, 3 * kt + kh, p, sub), stage, unit)
                     load = stage
                     for chunk, ref, index in users(kt, kh):
                         pltpu.matmul_acc_lhs(
@@ -201,7 +198,7 @@
 
 
 def inner_kernel(
-    x_ref, prev_ref, u0, u1, u2, par_ref, packed_ref, part_ref, ends_ref, gather, spread, a1, square, scale
+    x_ref, prev_ref, u_ref, par_ref, packed_ref, part_ref, ends_ref, gather, spread, a1, square, scale
 ):
     del packed_ref
     older = lax.axis_index("tm") > 0
@@ -228,15 +225,15 @@
             shifted(a1, f, g, v, none, none)
             ends_ref[0, f : f + 1, cut] = v[0:1]
             ends_ref[1, f : f + 1, cut] = v[15:16]
-    for p, w in enumerate((u0, u1, u2)):
-        totals = convolve(p, w, lambda kt, kh: [(f, a1, (kh, f + kt)) for f in range(6)], 6)
+    for p in range(3):
+        totals = convolve(p, u_ref, lambda kt, kh: [(f, a1, (kh, f + kt)) for f in range(6)], 6)
         for f, total in enumerate(totals):
             part_ref[64 * f : 64 * f + 64, pl.ds(256 * p, 256)] = total
 
 
 def main_kernel(
     x_ref, h0_ref, h1_ref, c_ref,
-    part_ref, ends_ref, gather, spread, u0, u1, u2, v0, v1, v2, par_ref, out_ref,
+    part_ref, ends_ref, gather, spread, u_ref, v_ref, par_ref, out_ref,
     square, scale, e, et, hid, a2,
 ):
     tm = lax.axis_index("tm")
@@ -285,7 +282,7 @@
                 ).astype(BF)
 
     spot = lax.broadcasted_iota(jnp.int32, (16, 256), 0)
-    for p, w in enumerate((u0, u1, u2)):
+    for p in range(3):
 
         def users(kt, kh):
             chunks = [(0, et, (kt, kh))]
@@ -294,7 +291,7 @@
             return chunks
 
         lanes = pl.ds(256 * p, 256)
-        outside, first, last = convolve(p, w, users, 3)
+        outside, first, last = convolve(p, u_ref, users, 3)
         bias = bias1[:, 256 * p : 256 * p + 256]
         for f in range(6):
             for g in range(4):
@@ -326,8 +323,8 @@
                 v = jnp.where(older, v, 0.0)
             shifted(a2, f, g, v, e[0, f : f + 1, cut], e[0, 8 + f : 9 + f, cut])
 
-    for p, w in enumerate((v0, v1, v2)):
-        totals = convolve(p, w, lambda kt, kh: [(f, a2, (kh, f + kt)) for f in range(4)], 4)
+    for p in range(3):
+        totals = convolve(p, v_ref, lambda kt, kh: [(f, a2, (kh, f + kt)) for f in range(4)], 4)
         for f, total in enumerate(totals):
             total = total + bias2[:, 256 * p : 256 * p + 256]
             for g in range(4):
@@ -371,7 +368,7 @@
             pltpu.VMEM((GROUP, 256), BF),
             pltpu.VMEM((256, GROUP), BF),
         ),
-        in_specs=[vmem()] * 7,
+        in_specs=[vmem()] * 5,
         out_specs=(vmem(),) * 4,
         scratch_shapes=[
             pltpu.VMEM((3, 8, 16, WIDE), BF),
@@ -416,7 +413,7 @@
     return pl.pallas_call(
         main_kernel,
         out_shape=jax.ShapeDtypeStruct((4, 16, LANES), BF),
-        in_specs=[vmem()] * 15,
+        in_specs=[vmem()] * 11,
         out_specs=vmem(),
         scratch_shapes=SCRATCH,
         compiler_params=pltpu.CompilerParams(vmem_limit_bytes=16 << 20),
@@ -434,9 +431,9 @@
         h0 = lax.ppermute(e0, axes, even_swap)
         h1 = lax.ppermute(e1, axes, odd_swap)
         banded = bands(weight_one, weight_two, (gain_one, bias_one, gain_two, bias_two))
-        packed = pack(h0, h1, banded[6])
+        packed = pack(h0, h1, banded[2])
         corners = lax.ppermute(packed, axes, later)
-        partial = inner(near, prev, *banded[:3], banded[6], packed)
+        partial = inner(near, prev, banded[0], banded[2], packed)
         return block(near, h0, h1, corners, *partial, *banded)
 
     in_specs = (P("tm", "rows", None), P(), P(), P(), P(), P(), P())

time: 23.7 us -> 23.8 us (level)
  no operation moved by 1% of the time
where the time goes in v4:
time: 23.8 us; the launch traced here: 23.6 us
  Pallas kernels  14.4 us (61%)
  waiting for transfers between devices  6.85 us (29%)
  starting transfers between devices  2.33 us (10%)
    pallas_call x1, Pallas kernels, block(): pl.pallas_call(main_kernel, out_shape=jax.ShapeDtypeStruct((4, 16, LANES)...  6.02 us
    pallas_call x1, Pallas kernels, inner(): pl.pallas_call(inner_kernel, out_shape=(pltpu.VMEM((384, GROUP), F32), pl...  4.67 us
    ppermute x1, waiting for transfers between devices, body(): h1 = lax.ppermute(e1, axes, odd_swap)  4.57 us
    pallas_call x1, Pallas kernels, bands(): pl.pallas_call(band_kernel, out_shape=(strip, strip, pltpu.VMEM((4, GROUP...  2.61 us
    ppermute x1, waiting for transfers between devices, body(): corners = lax.ppermute(packed, axes, later)  2.21 us
    ppermute x1, starting transfers between devices, body(): h0 = lax.ppermute(e0, axes, even_swap)  1.66 us
    pallas_call x1, Pallas kernels, fetch(): pl.pallas_call(fetch_kernel, out_shape=(edge, edge, pltpu.VMEM((4, 16, LA...  1.11 us
    ppermute x1, starting transfers between devices, body(): corners = lax.ppermute(packed, axes, later)  0.66 us
  transfers between devices with their start and end apart: 4, of which 3 were waited for; matrix products, arithmetic and copies ran while one was open for 0% of the time, Pallas kernels for 36%

profile of v4, /device:TPU:128, one launch (start us, length us, event | category | flops | bytes accessed | tf_op | source)
XLA Modules:
  0.0 23.6 jit_solution(1462748625694072791)
XLA Ops:
  0.0 0.0 collective-permute-start.3
  0.0 1.1 %fetch.1 = (bf16[8,3072]{1,0:T(8,128)(2,1)S(1)}, bf16[8,3072]{1,0:T(8,128)(2,1)S(1)}, bf16[4,16,3072]{2,1,0:T(8,128)(2,1)S(1)}) custom-call(bf16[4,16,3072]{2,1,0:T(8,128)(2,1)} %x_hbm.1), custom_call_target="tpu_custom_call" | custom-call | tf_op jit(solution)/shard_map/fetch/pallas_call | solution.py:42
  1.1 1.7 %collective-permute-start = (bf16[8,3072]{1,0:T(8,128)(2,1)S(1)}, bf16[8,3072]{1,0:T(8,128)(2,1)S(1)}, u32[]{:S(2)}, u32[]{:S(2)}) collective-permute-start(bf16[8,3072]{1,0:T(8,128)(2,1)S(1)} %get-tuple-element.16), channel_id=1, source_target_pairs={{0,1},{1,0},{2,3},{3,2},{4,5},{5,4},{6,7},{7,6},{8,9},{9,8},{10,11... | collective-permute-start | bytes 147464 | tf_op jit(solution)/shard_map/ppermute | solution.py:431
  2.8 0.0 collective-permute-start.1
  2.8 2.6 %bands.1 = (bf16[9,3,384,128]{3,2,1,0:T(8,128)(2,1)S(1)}, bf16[9,3,384,128]{3,2,1,0:T(8,128)(2,1)S(1)}, f32[4,768]{1,0:T(4,128)S(1)}) custom-call(bf16[27,96,96]{2,1,0:T(8,128)(2,1)} %bitcast.6, bf16[27,96,96]{2,1,0:T(8,128)(2,1)} %bitcast.7, f32[1,96]{1,0:T(1,128)} %bitcast.8, f32[1,96]{1,0:T(1,128)} %bitcast.9, f32[1,96]{1,0:T(1,128)} %bitcast.10, ...), custom_call_target="tpu_custom_call" | custom-call | flops 4000000000 | bytes 18000000 | tf_op jit(solution)/shard_map/bands/pallas_call | solution.py:106
  5.4 0.0 collective-permute-done.h0_ref
  5.4 4.6 %collective-permute-done.1.h1_ref = bf16[8,3072]{1,0:T(8,128)(2,1)S(1)} collective-permute-done((bf16[8,3072]{1,0:T(8,128)(2,1)S(1)}, bf16[8,3072]{1,0:T(8,128)(2,1)S(1)}, u32[]{:S(2)}, u32[]{:S(2)}) %collective-permute-start.1) | collective-permute-done | bytes 49184 | tf_op jit(solution)/shard_map/ppermute | solution.py:432
  10.0 0.7 %collective-permute-start.2 = (bf16[16,3072]{1,0:T(8,128)(2,1)S(1)}, bf16[16,3072]{1,0:T(8,128)(2,1)S(1)}, u32[]{:S(2)}, u32[]{:S(2)}) collective-permute-start(bf16[16,3072]{1,0:T(8,128)(2,1)S(1)} %pack.1.packed_ref), channel_id=1, source_target_pairs={{0,16},{1,17},{2,18},{3,19},{4,20},{5,21},{6,22},{7,23},{8,24},{9,... | collective-permute-start | bytes 294920 | tf_op jit(solution)/shard_map/ppermute | solution.py:435
  10.7 0.1 collective-permute-done.3.prev_ref
  10.7 4.7 %inner.1 = (f32[384,768]{1,0:T(8,128)S(1)}, f32[2,8,3072]{2,1,0:T(8,128)S(1)}, bf16[768,256]{1,0:T(8,128)(2,1)S(1)}, bf16[256,768]{1,0:T(8,128)(2,1)S(1)}) custom-call(bf16[4,16,3072]{2,1,0:T(8,128)(2,1)S(1)} %get-tuple-element.15.x_ref, bf16[4,16,3072]{2,1,0:T(8,128)(2,1)S(1)} %collective-permute-done.3.prev_ref, ...), custom_call_target="tpu_custom_call" | custom-call | flops 4000000000 | bytes 18000000 | tf_op jit(solution)/shard_map/inner/pallas_call | solution.py:363
  15.4 2.2 %collective-permute-done.2.c_ref = bf16[16,3072]{1,0:T(8,128)(2,1)S(1)} collective-permute-done((bf16[16,3072]{1,0:T(8,128)(2,1)S(1)}, bf16[16,3072]{1,0:T(8,128)(2,1)S(1)}, u32[]{:S(2)}, u32[]{:S(2)}) %collective-permute-start.2) | collective-permute-done | bytes 98336 | tf_op jit(solution)/shard_map/ppermute | solution.py:435
  17.6 6.0 %block.1 = bf16[4,16,3072]{2,1,0:T(8,128)(2,1)} custom-call(bf16[4,16,3072]{2,1,0:T(8,128)(2,1)S(1)} %get-tuple-element.15.x_ref, bf16[8,3072]{1,0:T(8,128)(2,1)S(1)} %collective-permute-done.h0_ref, bf16[8,3072]{1,0:T(8,128)(2,1)S(1)} %collective-permute-done.1.h1_ref, bf16[16,3072]{1,0:T(8,128)(2,1)S(1)} %collective-permute-done.2.c_ref, ...), custom_call_target="tpu_custom_call" | custom-call | tf_op jit(solution)/shard_map/block/pallas_call | solution.py:413
  (1 shorter events, 0.0 us)
Async XLA Ops:
  0.0 10.7 %collective-permute-start.3 = (bf16[4,16,3072]{2,1,0:T(8,128)(2,1)}, bf16[4,16,3072]{2,1,0:T(8,128)(2,1)S(1)}, u32[]{:S(2)}, u32[]{:S(2)}) collective-permute-start(bf16[4,16,3072]{2,1,0:T(8,128)(2,1)} %x_hbm.1), channel_id=1, source_target_pairs={{0,16},{1,17},{2,18},{3,19},{4,20},{5,21},{6,22},{7,23},{8,24},{9,... | collective-permute-start | bytes 1179656 | tf_op jit(solution)/shard_map/ppermute | solution.py:429
  1.1 4.3 %collective-permute-start = (bf16[8,3072]{1,0:T(8,128)(2,1)S(1)}, bf16[8,3072]{1,0:T(8,128)(2,1)S(1)}, u32[]{:S(2)}, u32[]{:S(2)}) collective-permute-start(bf16[8,3072]{1,0:T(8,128)(2,1)S(1)} %get-tuple-element.16), channel_id=1, source_target_pairs={{0,1},{1,0},{2,3},{3,2},{4,5},{5,4},{6,7},{7,6},{8,9},{9,8},{10,11... | collective-permute-start | bytes 147464 | tf_op jit(solution)/shard_map/ppermute | solution.py:431
  2.8 7.2 %collective-permute-start.1 = (bf16[8,3072]{1,0:T(8,128)(2,1)S(1)}, bf16[8,3072]{1,0:T(8,128)(2,1)S(1)}, u32[]{:S(2)}, u32[]{:S(2)}) collective-permute-start(bf16[8,3072]{1,0:T(8,128)(2,1)S(1)} %get-tuple-element.17), channel_id=1, source_target_pairs={{0,16},{1,2},{2,1},{3,4},{4,3},{5,6},{6,5},{7,8},{8,7},{9,10},{10,... | collective-permute-start | bytes 147464 | tf_op jit(solution)/shard_map/ppermute | solution.py:432
  10.0 7.6 %collective-permute-start.2 = (bf16[16,3072]{1,0:T(8,128)(2,1)S(1)}, bf16[16,3072]{1,0:T(8,128)(2,1)S(1)}, u32[]{:S(2)}, u32[]{:S(2)}) collective-permute-start(bf16[16,3072]{1,0:T(8,128)(2,1)S(1)} %pack.1.packed_ref), channel_id=1, source_target_pairs={{0,16},{1,17},{2,18},{3,19},{4,20},{5,21},{6,22},{7,23},{8,24},{9,... | collective-permute-start | bytes 294920 | tf_op jit(solution)/shard_map/ppermute | solution.py:435

commit v5 on v4

--- a/solution.py
+++ b/solution.py
@@ -138,20 +138,25 @@
             for unit in range(2):
                 pltpu.matmul_push_rhs(gather[256 * k : 256 * k + 256, :], k % 2, unit)
                 lhs = square[half * unit : half * unit + half, 256 * k : 256 * k + 256]
-                pltpu.matmul_acc_lhs(accs[unit], lhs, load_staged_rhs=k % 2)
+                pltpu.matmul_acc_lhs(accs[3 * unit], lhs, load_staged_rhs=k % 2)
+        left = []
         for unit in range(2):
-            total = pltpu.matmul_pop(accs[unit])[:, 0:128]
+            total = pltpu.matmul_pop(accs[3 * unit])[:, 0:128]
             r = lax.rsqrt(total * (1.0 / C) + 1e-06)
             high = r.astype(BF)
             low = (r - high.astype(F32)).astype(BF)
-            lhs = jnp.concatenate([high, low], axis=1)
-            for n in range(3):
+            left.append(jnp.concatenate([high, low], axis=1))
+        for n in range(3):
+            for unit in range(2):
                 stage = (n + 1) % 2
                 pltpu.matmul_push_rhs(spread[:, 256 * n : 256 * n + 256], stage, unit)
-                pltpu.matmul_acc_lhs(accs[unit], lhs, load_staged_rhs=stage)
-                scale[half * unit : half * unit + half, 256 * n : 256 * n + 256] = pltpu.matmul_pop(accs[unit])
-
-    pl.run_scoped(run, *[pltpu.ACC(n)((half, 256), F32) for n in range(2)])
+                pltpu.matmul_acc_lhs(accs[3 * unit + n], left[unit], load_staged_rhs=stage)
+        for n in range(3):
+            for unit in range(2):
+                rows = pl.ds(half * unit, half)
+                scale[rows, 256 * n : 256 * n + 256] = pltpu.matmul_pop(accs[3 * unit + n])
+
+    pl.run_scoped(run, *[pltpu.ACC(n // 3)((half, 256), F32) for n in range(6)])
 
 
 def act(v, scale, gain):
@@ -426,8 +431,8 @@
     axes = ("tm", "rows")
 
     def body(frames, gain_one, weight_one, bias_one, gain_two, weight_two, bias_two):
-        prev = lax.ppermute(frames, axes, later)
         e0, e1, near = fetch(frames)
+        prev = lax.ppermute(near, axes, later)
         h0 = lax.ppermute(e0, axes, even_swap)
         h1 = lax.ppermute(e1, axes, odd_swap)
         banded = bands(weight_one, weight_two, (gain_one, bias_one, gain_two, bias_two))

time: 23.8 us -> 24 us (level)
    ppermute x1, waiting for transfers between devices: 0.08 us -> 0.98 us  [body(): prev = lax.ppermute(near, axes, later)]
    ppermute x1, waiting for transfers between devices: 2.21 us -> 1.41 us  [body(): corners = lax.ppermute(packed, axes, later)]
  transfers between devices with their start and end apart: 4 -> 4, of which waited for: 3 -> 3; matrix products, arithmetic and copies ran while one was open for 0% -> 0% of each run, Pallas kernels for 36% -> 30%
where the time goes in v5:
time: 24 us; the launch traced here: 23.8 us
  Pallas kernels  14.4 us (60%)
  waiting for transfers between devices  7.02 us (29%)
  starting transfers between devices  2.34 us (10%)
    pallas_call x1, Pallas kernels, block(): pl.pallas_call(main_kernel, out_shape=jax.ShapeDtypeStruct((4, 16, LANES)...  6.05 us
    pallas_call x1, Pallas kernels, inner(): pl.pallas_call(inner_kernel, out_shape=(pltpu.VMEM((384, GROUP), F32), pl...  4.63 us
    ppermute x1, waiting for transfers between devices, body(): h1 = lax.ppermute(e1, axes, odd_swap)  4.63 us
    pallas_call x1, Pallas kernels, bands(): pl.pallas_call(band_kernel, out_shape=(strip, strip, pltpu.VMEM((4, GROUP...  2.61 us
    ppermute x1, starting transfers between devices, body(): h0 = lax.ppermute(e0, axes, even_swap)  1.66 us
    ppermute x1, waiting for transfers between devices, body(): corners = lax.ppermute(packed, axes, later)  1.41 us
    pallas_call x1, Pallas kernels, fetch(): pl.pallas_call(fetch_kernel, out_shape=(edge, edge, pltpu.VMEM((4, 16, LA...  1.11 us
    ppermute x1, waiting for transfers between devices, body(): prev = lax.ppermute(near, axes, later)  0.98 us
  transfers between devices with their start and end apart: 4, of which 3 were waited for; matrix products, arithmetic and copies ran while one was open for 0% of the time, Pallas kernels for 30%

profile of v5, /device:TPU:128, one launch (start us, length us, event | category | flops | bytes accessed | tf_op | source)
XLA Modules:
  0.0 23.8 jit_solution(5640257319802974625)
XLA Ops:
  0.0 1.1 %fetch.1 = (bf16[8,3072]{1,0:T(8,128)(2,1)S(1)}, bf16[8,3072]{1,0:T(8,128)(2,1)S(1)}, bf16[4,16,3072]{2,1,0:T(8,128)(2,1)S(1)}) custom-call(bf16[4,16,3072]{2,1,0:T(8,128)(2,1)} %x_hbm.1), custom_call_target="tpu_custom_call" | custom-call | tf_op jit(solution)/shard_map/fetch/pallas_call | solution.py:42
  1.1 0.1 collective-permute-start.3
  1.2 1.7 %collective-permute-start = (bf16[8,3072]{1,0:T(8,128)(2,1)S(1)}, bf16[8,3072]{1,0:T(8,128)(2,1)S(1)}, u32[]{:S(2)}, u32[]{:S(2)}) collective-permute-start(bf16[8,3072]{1,0:T(8,128)(2,1)S(1)} %get-tuple-element.16), channel_id=1, source_target_pairs={{0,1},{1,0},{2,3},{3,2},{4,5},{5,4},{6,7},{7,6},{8,9},{9,8},{10,11... | collective-permute-start | bytes 147464 | tf_op jit(solution)/shard_map/ppermute | solution.py:436
  2.9 0.0 collective-permute-start.1
  2.9 2.6 %bands.1 = (bf16[9,3,384,128]{3,2,1,0:T(8,128)(2,1)S(1)}, bf16[9,3,384,128]{3,2,1,0:T(8,128)(2,1)S(1)}, f32[4,768]{1,0:T(4,128)S(1)}) custom-call(bf16[27,96,96]{2,1,0:T(8,128)(2,1)} %bitcast.6, bf16[27,96,96]{2,1,0:T(8,128)(2,1)} %bitcast.7, f32[1,96]{1,0:T(1,128)} %bitcast.8, f32[1,96]{1,0:T(1,128)} %bitcast.9, f32[1,96]{1,0:T(1,128)} %bitcast.10, ...), custom_call_target="tpu_custom_call" | custom-call | flops 4000000000 | bytes 18000000 | tf_op jit(solution)/shard_map/bands/pallas_call | solution.py:106
  5.5 0.0 collective-permute-done.h0_ref
  5.5 4.6 %collective-permute-done.1.h1_ref = bf16[8,3072]{1,0:T(8,128)(2,1)S(1)} collective-permute-done((bf16[8,3072]{1,0:T(8,128)(2,1)S(1)}, bf16[8,3072]{1,0:T(8,128)(2,1)S(1)}, u32[]{:S(2)}, u32[]{:S(2)}) %collective-permute-start.1) | collective-permute-done | bytes 49184 | tf_op jit(solution)/shard_map/ppermute | solution.py:437
  10.2 0.6 %collective-permute-start.2 = (bf16[16,3072]{1,0:T(8,128)(2,1)S(1)}, bf16[16,3072]{1,0:T(8,128)(2,1)S(1)}, u32[]{:S(2)}, u32[]{:S(2)}) collective-permute-start(bf16[16,3072]{1,0:T(8,128)(2,1)S(1)} %pack.1.packed_ref), channel_id=1, source_target_pairs={{0,16},{1,17},{2,18},{3,19},{4,20},{5,21},{6,22},{7,23},{8,24},{9,... | collective-permute-start | bytes 294920 | tf_op jit(solution)/shard_map/ppermute | solution.py:440
  10.7 1.0 %collective-permute-done.3.prev_ref = bf16[4,16,3072]{2,1,0:T(8,128)(2,1)S(1)} collective-permute-done((bf16[4,16,3072]{2,1,0:T(8,128)(2,1)S(1)}, bf16[4,16,3072]{2,1,0:T(8,128)(2,1)S(1)}, u32[]{:S(2)}, u32[]{:S(2)}) %collective-permute-start.3) | collective-permute-done | bytes 393248 | tf_op jit(solution)/shard_map/ppermute | solution.py:435
  11.7 4.6 %inner.1 = (f32[384,768]{1,0:T(8,128)S(1)}, f32[2,8,3072]{2,1,0:T(8,128)S(1)}, bf16[768,256]{1,0:T(8,128)(2,1)S(1)}, bf16[256,768]{1,0:T(8,128)(2,1)S(1)}) custom-call(bf16[4,16,3072]{2,1,0:T(8,128)(2,1)S(1)} %get-tuple-element.15.x_ref, bf16[4,16,3072]{2,1,0:T(8,128)(2,1)S(1)} %collective-permute-done.3.prev_ref, ...), custom_call_target="tpu_custom_call" | custom-call | flops 4000000000 | bytes 18000000 | tf_op jit(solution)/shard_map/inner/pallas_call | solution.py:368
  16.4 1.4 %collective-permute-done.2.c_ref = bf16[16,3072]{1,0:T(8,128)(2,1)S(1)} collective-permute-done((bf16[16,3072]{1,0:T(8,128)(2,1)S(1)}, bf16[16,3072]{1,0:T(8,128)(2,1)S(1)}, u32[]{:S(2)}, u32[]{:S(2)}) %collective-permute-start.2) | collective-permute-done | bytes 98336 | tf_op jit(solution)/shard_map/ppermute | solution.py:440
  17.8 6.1 %block.1 = bf16[4,16,3072]{2,1,0:T(8,128)(2,1)} custom-call(bf16[4,16,3072]{2,1,0:T(8,128)(2,1)S(1)} %get-tuple-element.15.x_ref, bf16[8,3072]{1,0:T(8,128)(2,1)S(1)} %collective-permute-done.h0_ref, bf16[8,3072]{1,0:T(8,128)(2,1)S(1)} %collective-permute-done.1.h1_ref, bf16[16,3072]{1,0:T(8,128)(2,1)S(1)} %collective-permute-done.2.c_ref, ...), custom_call_target="tpu_custom_call" | custom-call | tf_op jit(solution)/shard_map/block/pallas_call | solution.py:418
  (1 shorter events, 0.0 us)
Async XLA Ops:
  1.1 10.6 %collective-permute-start.3 = (bf16[4,16,3072]{2,1,0:T(8,128)(2,1)S(1)}, bf16[4,16,3072]{2,1,0:T(8,128)(2,1)S(1)}, u32[]{:S(2)}, u32[]{:S(2)}) collective-permute-start(bf16[4,16,3072]{2,1,0:T(8,128)(2,1)S(1)} %get-tuple-element.15.x_ref), channel_id=1, source_target_pairs={{0,16},{1,17},{2,18},{3,19},{4,20},{5,21},{6,22},{7,23},{8,24},{9,... | collective-permute-start | bytes 1179656 | tf_op jit(solution)/shard_map/ppermute | solution.py:435
  1.2 4.3 %collective-permute-start = (bf16[8,3072]{1,0:T(8,128)(2,1)S(1)}, bf16[8,3072]{1,0:T(8,128)(2,1)S(1)}, u32[]{:S(2)}, u32[]{:S(2)}) collective-permute-start(bf16[8,3072]{1,0:T(8,128)(2,1)S(1)} %get-tuple-element.16), channel_id=1, source_target_pairs={{0,1},{1,0},{2,3},{3,2},{4,5},{5,4},{6,7},{7,6},{8,9},{9,8},{10,11... | collective-permute-start | bytes 147464 | tf_op jit(solution)/shard_map/ppermute | solution.py:436
  2.9 7.3 %collective-permute-start.1 = (bf16[8,3072]{1,0:T(8,128)(2,1)S(1)}, bf16[8,3072]{1,0:T(8,128)(2,1)S(1)}, u32[]{:S(2)}, u32[]{:S(2)}) collective-permute-start(bf16[8,3072]{1,0:T(8,128)(2,1)S(1)} %get-tuple-element.17), channel_id=1, source_target_pairs={{0,16},{1,2},{2,1},{3,4},{4,3},{5,6},{6,5},{7,8},{8,7},{9,10},{10,... | collective-permute-start | bytes 147464 | tf_op jit(solution)/shard_map/ppermute | solution.py:437
  10.2 7.6 %collective-permute-start.2 = (bf16[16,3072]{1,0:T(8,128)(2,1)S(1)}, bf16[16,3072]{1,0:T(8,128)(2,1)S(1)}, u32[]{:S(2)}, u32[]{:S(2)}) collective-permute-start(bf16[16,3072]{1,0:T(8,128)(2,1)S(1)} %pack.1.packed_ref), channel_id=1, source_target_pairs={{0,16},{1,17},{2,18},{3,19},{4,20},{5,21},{6,22},{7,23},{8,24},{9,... | collective-permute-start | bytes 294920 | tf_op jit(solution)/shard_map/ppermute | solution.py:440
